TPU v7x, 128 devices: a whole 4x4x4 slice. The times are simulated.
128 devices in a mesh: cam: 8 (over x, core), band: 16 (over z, y).
Axes of the slice: x: 4, y: 4, z: 4, core: 2. Of those that a mesh axis runs over, the one named last changes fastest.
Arguments:
- query: bfloat16 [65536, 256], P(('cam', 'band')), may hold values from -6 to 6
- key_img: bfloat16 [8, 16384, 256], P('cam', 'band'), may hold values from -6 to 6
- value_img: bfloat16 [8, 16384, 256], P('cam', 'band'), may hold values from -6 to 6
- d_out: bfloat16 [65536, 256], P(('cam', 'band')), may hold values from -12 to 12
- visible: int32 [128, 6], replicated, may hold values from 0 to 255, as said below
Outputs:
- d_query: bfloat16 [65536, 256], P(('cam', 'band'))
- d_key: bfloat16 [8, 16384, 256], P('cam', 'band')
- d_value: bfloat16 [8, 16384, 256], P('cam', 'band')
Inputs may be any that keep to these rules, and one draw needn't show every extreme that they name: `visible`: row t names 6 different blocks, each of camera t // 16 or of camera (t // 16 + 1) mod 8, and at most one block of each row band.
All inputs are finite; a program needn't handle non-finite values.
Results may differ from a plain program's by a relative error of at most 0.013.
The roundings to bfloat16 on the way count: a program that leaves them out, or rounds other values in their place, can miss the bound.
Values may be sent and summed in bfloat16 or wider, within the bound.
A program may use at most 192 MiB of HBM per device.

v0:
```python
import jax
import jax.numpy as jnp
from jax import lax
from jax.sharding import PartitionSpec as P

HEADS = 8
BLOCK = 512


def from_behind(x, axis, by):
    length = lax.axis_size(axis)
    return lax.ppermute(x, axis, [(i, (i + by) % length) for i in range(length)])


def block_scores(queries, block_keys):
    factor = queries.shape[2] ** (-0.5)
    return (
        jnp.einsum("qhd,khd->hqk", queries, block_keys, preferred_element_type=jnp.float32) * factor
    )


def block_terms(queries, grads, logsum, delta, block_keys, block_values):
    probs = jnp.exp(block_scores(queries, block_keys) - logsum[..., None])
    probs_low = probs.astype(jnp.bfloat16)
    dprob = jnp.einsum("qhd,khd->hqk", grads, block_values, preferred_element_type=jnp.float32)
    dscore = (probs * (dprob - delta[..., None])).astype(jnp.bfloat16)
    return (probs_low, dscore)


def key_value_grads(queries, grads, probs_low, dscore):
    factor = queries.shape[2] ** (-0.5)
    grad_key = (
        jnp.einsum("hqk,qhd->khd", dscore, queries, preferred_element_type=jnp.float32) * factor
    )
    grad_value = jnp.einsum("hqk,qhd->khd", probs_low, grads, preferred_element_type=jnp.float32)
    return (grad_key, grad_value)


def local(query, key_img, value_img, d_out, visible):
    camera_count = lax.axis_size("cam")
    band_count = lax.axis_size("band")
    cam_index = lax.axis_index("cam")
    band_index = lax.axis_index("band")
    width = key_img.shape[2]
    head_dim = width // HEADS
    per_device = key_img.shape[1] // BLOCK
    row_count = query.shape[0]
    own_keys = key_img.reshape(per_device, BLOCK, width)
    own_values = value_img.reshape(per_device, BLOCK, width)
    next_keys, next_values = from_behind((own_keys, own_values), "cam", -1)
    pair_keys = jnp.concatenate([own_keys, next_keys], axis=0)
    pair_values = jnp.concatenate([own_values, next_values], axis=0)
    group = lax.dynamic_slice_in_dim(visible, cam_index * band_count, band_count, 0)
    owner_ids = group // per_device
    group_band = owner_ids % band_count
    group_local = (
        owner_ids // band_count - cam_index
    ) % camera_count * per_device + group % per_device
    asked = group_band == band_index
    wanted = jnp.sum(jnp.where(asked, group_local, 0), axis=1)
    served = jnp.any(asked, axis=1)
    send_keys = jnp.take(pair_keys, wanted, axis=0)
    send_values = jnp.take(pair_values, wanted, axis=0)
    recv_keys, recv_values = (
        lax.all_to_all(send_keys, "band", split_axis=0, concat_axis=0, tiled=True),
        lax.all_to_all(send_values, "band", split_axis=0, concat_axis=0, tiled=True),
    )
    list_band = lax.dynamic_index_in_dim(group_band, band_index, 0, keepdims=False)
    tile_keys = jnp.take(recv_keys, list_band, axis=0).reshape(-1, BLOCK, HEADS, head_dim)
    tile_values = jnp.take(recv_values, list_band, axis=0).reshape(-1, BLOCK, HEADS, head_dim)
    slot_count = tile_keys.shape[0]
    queries = query.reshape(row_count, HEADS, head_dim)
    grads = d_out.reshape(row_count, HEADS, head_dim)
    running_max = jnp.full((HEADS, row_count), -jnp.inf, jnp.float32)
    running_sum = jnp.zeros((HEADS, row_count), jnp.float32)
    for slot_index in range(slot_count):
        scores = block_scores(queries, tile_keys[slot_index])
        new_max = jnp.maximum(running_max, jnp.max(scores, axis=-1))
        running_sum = running_sum * jnp.exp(running_max - new_max) + jnp.sum(
            jnp.exp(scores - new_max[..., None]), axis=-1
        )
        running_max = new_max
    logsum = running_max + jnp.log(running_sum)
    attended = jnp.zeros((row_count, HEADS, head_dim), jnp.float32)
    for slot_index in range(slot_count):
        probs_low = jnp.exp(
            block_scores(queries, tile_keys[slot_index]) - logsum[..., None]
        ).astype(jnp.bfloat16)
        attended = attended + jnp.einsum(
            "hqk,khd->qhd", probs_low, tile_values[slot_index], preferred_element_type=jnp.float32
        )
    delta = jnp.sum(grads.astype(jnp.float32) * attended, axis=-1).T
    dquery = jnp.zeros((row_count, HEADS, head_dim), jnp.float32)
    key_parts = []
    value_parts = []
    for slot_index in range(slot_count):
        probs_low, dscore = block_terms(
            queries, grads, logsum, delta, tile_keys[slot_index], tile_values[slot_index]
        )
        dquery = dquery + jnp.einsum(
            "hqk,khd->qhd", dscore, tile_keys[slot_index], preferred_element_type=jnp.float32
        )
        grad_key, grad_value = key_value_grads(queries, grads, probs_low, dscore)
        key_parts.append(grad_key.reshape(BLOCK, width))
        value_parts.append(grad_value.reshape(BLOCK, width))
    slot_keys = (
        jnp.zeros((band_count, BLOCK, width), jnp.float32).at[list_band].set(jnp.stack(key_parts))
    )
    slot_values = (
        jnp.zeros((band_count, BLOCK, width), jnp.float32).at[list_band].set(jnp.stack(value_parts))
    )
    back_keys, back_values = (
        lax.all_to_all(
            slot_keys.astype(jnp.bfloat16), "band", split_axis=0, concat_axis=0, tiled=True
        ).astype(slot_keys.dtype),
        lax.all_to_all(
            slot_values.astype(jnp.bfloat16), "band", split_axis=0, concat_axis=0, tiled=True
        ).astype(slot_values.dtype),
    )
    select = ((wanted[None, :] == jnp.arange(2 * per_device)[:, None]) & served[None, :]).astype(
        jnp.float32
    )
    pair_grad_keys = jnp.einsum("ij,jrd->ird", select, back_keys, precision=lax.Precision.HIGHEST)
    pair_grad_values = jnp.einsum(
        "ij,jrd->ird", select, back_values, precision=lax.Precision.HIGHEST
    )
    came_keys, came_values = (
        from_behind(pair_grad_keys[per_device:].astype(jnp.bfloat16), "cam", 1).astype(jnp.float32),
        from_behind(pair_grad_values[per_device:].astype(jnp.bfloat16), "cam", 1).astype(
            jnp.float32
        ),
    )
    d_key = (
        (pair_grad_keys[:per_device] + came_keys)
        .astype(jnp.bfloat16)
        .reshape(1, per_device * BLOCK, width)
    )
    d_value = (
        (pair_grad_values[:per_device] + came_values)
        .astype(jnp.bfloat16)
        .reshape(1, per_device * BLOCK, width)
    )
    d_query = (dquery * head_dim ** (-0.5)).astype(jnp.bfloat16).reshape(row_count, width)
    return (d_query, d_key, d_value)


def solution(mesh):
    in_specs = (
        P(("cam", "band"), None),
        P("cam", "band", None),
        P("cam", "band", None),
        P(("cam", "band"), None),
        P(),
    )
    out_specs = (P(("cam", "band"), None), P("cam", "band", None), P("cam", "band", None))
    return jax.shard_map(local, mesh=mesh, in_specs=in_specs, out_specs=out_specs, check_vma=False)
```

profile of v0, /device:TPU:1, one launch (start us, length us, event | category | flops | bytes accessed | tf_op | source)
XLA Modules:
  0.0 442.2 jit_solution(2706300609364528095)
XLA Ops:
  0.6 1.4 collective-permute-start
  2.1 2.3 collective-permute-start.1
  6.5 3.8 collective-permute-done
  11.5 2.8 gather_fusion
  14.3 1.7 collective-permute-done.1
  16.0 2.8 gather_fusion.2
  18.9 6.3 %broadcast_select_fusion = (bf16[16,512,256]{2,1,0:T(8,128)(2,1)}, bf16[16,512,256]{2,1,0:T(8,128)(2,1)S(1)}) fusion(bf16[16,512,256]{2,1,0:T(8,128)(2,1)} %gather_fusion.2, pred[16]{0:T(512)(128)(4,1)S(1)} %compare_and_fusion.1, bf16[16,512,256]{2,1,0:T(8,128)(2,1)} %gather_fusion), kind=kLoop, calls=%fused_computation.64 | loop fusion | flops 4194304 | bytes 16777232 | tf_op jit(solution)/shard_map/jit(_take)/select_n | solution.py:63
  25.1 57.4 %all_to_all.20 = bf16[16,512,256]{2,1,0:T(8,128)(2,1)} all-to-all(bf16[16,512,256]{2,1,0:T(8,128)(2,1)S(1)} %get-tuple-element.41), channel_id=1, replica_groups=mesh['cam'=8,'band'=16] {'band'}, dimensions={0} | all-to-all | bytes 8388608 | tf_op jit(solution)/shard_map/all_to_all | solution.py:65
  82.5 4.8 %all-to-all-start.1 = ((bf16[16,512,256]{2,1,0:T(8,128)(2,1)}), bf16[16,512,256]{2,1,0:T(8,128)(2,1)}, u32[]{:S(2)}, u32[]{:S(2)}) async-start(bf16[16,512,256]{2,1,0:T(8,128)(2,1)} %get-tuple-element.40), calls=%async_computation.1 | async-start | bytes 8388608 | tf_op jit(solution)/shard_map/all_to_all | solution.py:66
  87.8 2.8 gather_fusion.1
  90.7 55.4 %all-to-all-done.1 = bf16[16,512,256]{2,1,0:T(8,128)(2,1)} async-done(((bf16[16,512,256]{2,1,0:T(8,128)(2,1)}), bf16[16,512,256]{2,1,0:T(8,128)(2,1)}, u32[]{:S(2)}, u32[]{:S(2)}) %all-to-all-start.1) | async-done | bytes 4194336 | tf_op jit(solution)/shard_map/all_to_all | solution.py:66
  146.0 4.0 gather_fusion.3
  150.1 1.8 broadcast_select_fusion.2
  153.3 4.6 %bitcast_reduce_fusion = (f32[8,512]{1,0:T(8,128)S(1)}, f32[8,512,512]{2,1,0:T(8,128)}) fusion(bf16[512,8,32]{0,2,1:T(8,128)(2,1)S(1)} %bitcast.305, bf16[512,8,32]{0,2,1:T(8,128)(2,1)S(1)} %bitcast.293), kind=kOutput, calls=%fused_computation.20 | convolution fusion | flops 138407936 | bytes 8929280 | tf_op jit(solution)/shard_map/qhd,khd->hqk/dot_general | solution.py:18
  157.9 4.6 %bitcast_reduce_fusion.1 = (f32[8,512]{1,0:T(8,128)S(1)}, f32[8,512,512]{2,1,0:T(8,128)}) fusion(bf16[512,8,32]{0,2,1:T(8,128)(2,1)S(1)} %bitcast.321, bf16[512,8,32]{0,2,1:T(8,128)(2,1)S(1)} %bitcast.294), kind=kOutput, calls=%fused_computation.26 | convolution fusion | flops 138407936 | bytes 8929280 | tf_op jit(solution)/shard_map/qhd,khd->hqk/dot_general | solution.py:18
  162.6 4.6 %bitcast_reduce_fusion.2 = (f32[8,512]{1,0:T(8,128)S(1)}, f32[8,512,512]{2,1,0:T(8,128)}) fusion(bf16[512,8,32]{0,2,1:T(8,128)(2,1)S(1)} %bitcast.323, bf16[512,8,32]{0,2,1:T(8,128)(2,1)S(1)} %bitcast.295), kind=kOutput, calls=%fused_computation.32 | convolution fusion | flops 138407936 | bytes 8929280 | tf_op jit(solution)/shard_map/qhd,khd->hqk/dot_general | solution.py:18
  167.3 4.5 %bitcast_reduce_fusion.3 = (f32[8,512]{1,0:T(8,128)S(1)}, f32[8,512,512]{2,1,0:T(8,128)}) fusion(bf16[512,8,32]{0,2,1:T(8,128)(2,1)S(1)} %bitcast.325, bf16[512,8,32]{0,2,1:T(8,128)(2,1)S(1)} %bitcast.296), kind=kOutput, calls=%fused_computation.38 | convolution fusion | flops 138407936 | bytes 8929280 | tf_op jit(solution)/shard_map/qhd,khd->hqk/dot_general | solution.py:18
  172.0 4.5 %bitcast_reduce_fusion.5 = (f32[8,512]{1,0:T(8,128)S(1)}, f32[8,512,512]{2,1,0:T(8,128)}) fusion(bf16[512,8,32]{0,2,1:T(8,128)(2,1)S(1)} %bitcast.307, bf16[512,8,32]{0,2,1:T(8,128)(2,1)S(1)} %bitcast.297), kind=kOutput, calls=%fused_computation.50 | convolution fusion | flops 138407936 | bytes 8929280 | tf_op jit(solution)/shard_map/qhd,khd->hqk/dot_general | solution.py:18
  177.4 2.4 bitcast_reduce_fusion.4
  181.0 1.4 fusion.22
  182.4 1.8 fusion.19
  188.7 1.4 fusion.13
  195.2 5.7 %fusion.56 = f32[8,512,32]{1,2,0:T(8,128)} fusion(bf16[512,8,32]{0,2,1:T(8,128)(2,1)S(1)} %bitcast.280, f32[8,512,512]{2,1,0:T(8,128)} %get-tuple-element.51, f32[8,512]{1,0:T(8,128)S(1)} %log_add_fusion), kind=kOutput, calls=%fused_computation.102 | convolution fusion | flops 140509184 | bytes 9191424 | tf_op jit(solution)/shard_map/hqk,qhd->khd/dot_general | solution.py:35
  200.9 5.7 %fusion.53 = f32[8,512,32]{1,2,0:T(8,128)} fusion(bf16[512,8,32]{0,2,1:T(8,128)(2,1)S(1)} %bitcast.281, f32[8,512,512]{2,1,0:T(8,128)} %copy-done.1, f32[8,512]{1,0:T(8,128)S(1)} %log_add_fusion), kind=kOutput, calls=%fused_computation.101 | convolution fusion | flops 140509184 | bytes 9191424 | tf_op jit(solution)/shard_map/hqk,qhd->khd/dot_general | solution.py:35
  206.6 5.7 %fusion.50 = f32[8,512,32]{1,2,0:T(8,128)} fusion(bf16[512,8,32]{0,2,1:T(8,128)(2,1)S(1)} %bitcast.282, f32[8,512,512]{2,1,0:T(8,128)} %get-tuple-element.49, f32[8,512]{1,0:T(8,128)S(1)} %log_add_fusion), kind=kOutput, calls=%fused_computation.100 | convolution fusion | flops 140509184 | bytes 9191424 | tf_op jit(solution)/shard_map/hqk,qhd->khd/dot_general | solution.py:35
  212.3 2.3 fusion.47
  214.6 2.5 fusion.44
  217.1 2.3 fusion.41
  219.6 4.9 %fusion.58 = f32[8,32,512]{2,1,0:T(8,128)S(1)} fusion(bf16[512,8,32]{0,2,1:T(8,128)(2,1)S(1)} %bitcast.315, f32[8,512,512]{2,1,0:T(8,128)} %get-tuple-element.51, f32[8,512]{1,0:T(8,128)S(1)} %log_add_fusion), kind=kOutput, calls=%fused_computation.103 | convolution fusion | flops 140509184 | bytes 9191424 | tf_op jit(solution)/shard_map/hqk,khd->qhd/dot_general | solution.py:89
  225.2 4.9 %convolution_add_fusion.9 = f32[8,32,512]{2,1,0:T(8,128)S(1)} fusion(f32[8,32,512]{2,1,0:T(8,128)S(1)} %fusion.58, bf16[512,8,32]{0,2,1:T(8,128)(2,1)S(1)} %bitcast.319, f32[8,512,512]{2,1,0:T(8,128)} %copy-done.1, f32[8,512]{1,0:T(8,128)S(1)} %log_add_fusion), kind=kOutput, calls=%fused_computation.86 | convolution fusion | flops 140640256 | bytes 9715712 | tf_op jit(solution)/shard_map/hqk,khd->qhd/dot_general | solution.py:89
  230.1 5.1 %convolution_add_fusion.8 = f32[8,32,512]{2,1,0:T(8,128)S(1)} fusion(f32[8,32,512]{2,1,0:T(8,128)S(1)} %convolution_add_fusion.9, bf16[512,8,32]{0,2,1:T(8,128)(2,1)S(1)} %bitcast.317, f32[8,512,512]{2,1,0:T(8,128)} %get-tuple-element.49, f32[8,512]{1,0:T(8,128)S(1)} %log_add_fusion), kind=kOutput, calls=%fused_computation.85 | convolution fusion | flops 140640256 | bytes 9715712 | tf_op jit(solution)/shard_map/hqk,khd->qhd/dot_general | solution.py:89
  235.2 5.0 %convolution_add_fusion.7 = f32[8,32,512]{2,1,0:T(8,128)S(1)} fusion(f32[8,32,512]{2,1,0:T(8,128)S(1)} %convolution_add_fusion.8, bf16[512,8,32]{0,2,1:T(8,128)(2,1)S(1)} %bitcast.313, f32[8,512,512]{2,1,0:T(8,128)} %get-tuple-element.47, f32[8,512]{1,0:T(8,128)S(1)} %log_add_fusion), kind=kOutput, calls=%fused_computation.84 | convolution fusion | flops 140640256 | bytes 9715712 | tf_op jit(solution)/shard_map/hqk,khd->qhd/dot_general | solution.py:89
  240.3 1.5 convolution_add_fusion.6
  242.7 1.6 fusion.38
  244.3 6.3 %fusion.4 = bf16[8,512,512]{1,2,0:T(8,128)(2,1)} fusion(f32[8,512,512]{2,1,0:T(8,128)} %copy-done.1, f32[8,512]{1,0:T(8,128)S(1)} %bitcast.342, f32[8,512]{1,0:T(8,128)S(1)} %log_add_fusion, bf16[512,8,32]{0,2,1:T(8,128)(2,1)S(1)} %bitcast.320, bf16[512,8,32]{0,2,1:T(8,128)(2,1)S(1)} %bitcast.287), kind=kOutput, calls=%fused_computation.15 | convolution fusion | flops 144703488 | bytes 13139968 | tf_op jit(solution)/shard_map/qhd,khd->hqk/dot_general | solution.py:25
  250.6 3.8 fusion.5
  254.6 3.8 fusion.3
  263.4 3.5 copy.205
  266.9 4.1 broadcast.114.clone.1
  271.0 7.2 %scatter_fusion.1 = f32[16,512,256]{2,1,0:T(8,128)} fusion(f32[16,512,256]{2,1,0:T(8,128)} %broadcast.114.clone.1, s32[6]{0:T(128)S(1)} %fusion.72, f32[6,512,256]{2,1,0:T(8,128)} %copy.205), kind=kCustom, calls=%fused_computation.5 | custom fusion | bytes 9437208 | tf_op jit(solution)/shard_map/scatter | solution.py:110
  278.2 5.9 %convert_element_type.88 = bf16[16,512,256]{2,1,0:T(8,128)(2,1)} convert(f32[16,512,256]{2,1,0:T(8,128)} %scatter_fusion.1) | non-fusion elementwise | flops 2097152 | bytes 12582912 | tf_op jit(solution)/shard_map/convert_element_type | solution.py:117
  284.1 4.6 %all-to-all-start.3 = ((bf16[16,512,256]{2,1,0:T(8,128)(2,1)}), bf16[16,512,256]{2,1,0:T(8,128)(2,1)}, u32[]{:S(2)}, u32[]{:S(2)}) async-start(bf16[16,512,256]{2,1,0:T(8,128)(2,1)} %convert_element_type.88), calls=%async_computation.3 | async-start | bytes 8388608 | tf_op jit(solution)/shard_map/all_to_all | solution.py:116
  288.7 3.5 convolution_multiply_fusion.4
  293.2 3.5 convolution_multiply_fusion.5
  297.7 3.5 convolution_multiply_fusion.3
  302.2 4.7 %fusion.2 = bf16[8,512,512]{1,2,0:T(8,128)(2,1)S(1)} fusion(f32[8,512,512]{2,1,0:T(8,128)} %get-tuple-element.47, f32[8,512]{1,0:T(8,128)S(1)} %bitcast.345, f32[8,512]{1,0:T(8,128)S(1)} %log_add_fusion, bf16[512,8,32]{0,2,1:T(8,128)(2,1)S(1)} %bitcast.314, bf16[512,8,32]{0,2,1:T(8,128)(2,1)S(1)} %bitcast.290), kind=kOutput, calls=%fused_computation.11 | convolution fusion | flops 144703488 | bytes 13139968 | tf_op jit(solution)/shard_map/qhd,khd->hqk/dot_general | solution.py:25
  306.9 2.0 copy-done.5
  311.2 4.7 %fusion.1 = bf16[8,512,512]{1,2,0:T(8,128)(2,1)S(1)} fusion(f32[8,512,512]{2,1,0:T(8,128)} %get-tuple-element.45, f32[8,512]{1,0:T(8,128)S(1)} %bitcast.346, f32[8,512]{1,0:T(8,128)S(1)} %log_add_fusion, bf16[512,8,32]{0,2,1:T(8,128)(2,1)S(1)} %bitcast.312, bf16[512,8,32]{0,2,1:T(8,128)(2,1)S(1)} %bitcast.291), kind=kOutput, calls=%fused_computation.9 | convolution fusion | flops 144703488 | bytes 13139968 | tf_op jit(solution)/shard_map/qhd,khd->hqk/dot_general | solution.py:25
  315.9 2.0 copy-done.7
  320.2 4.7 %fusion = bf16[8,512,512]{1,2,0:T(8,128)(2,1)S(1)} fusion(f32[8,512,512]{2,1,0:T(8,128)} %get-tuple-element.43, f32[8,512]{1,0:T(8,128)S(1)} %bitcast.347, f32[8,512]{1,0:T(8,128)S(1)} %log_add_fusion, bf16[512,8,32]{0,2,1:T(8,128)(2,1)S(1)} %bitcast.310, bf16[512,8,32]{0,2,1:T(8,128)(2,1)S(1)} %bitcast.292), kind=kOutput, calls=%fused_computation.7 | convolution fusion | flops 144703488 | bytes 13139968 | tf_op jit(solution)/shard_map/qhd,khd->hqk/dot_general | solution.py:25
  334.3 4.1 broadcast.114.clone
  338.5 6.2 %scatter_fusion = f32[16,512,256]{2,1,0:T(8,128)} fusion(f32[16,512,256]{2,1,0:T(8,128)} %broadcast.114.clone, s32[6]{0:T(128)S(1)} %fusion.72, f32[6,512,256]{2,1,0:T(8,128)S(1)} %constant_dynamic-update-slice_fusion), kind=kCustom, calls=%fused_computation.4 | custom fusion | bytes 9437208 | tf_op jit(solution)/shard_map/scatter | solution.py:107
  344.7 5.9 %convert_element_type.85 = bf16[16,512,256]{2,1,0:T(8,128)(2,1)} convert(f32[16,512,256]{2,1,0:T(8,128)} %scatter_fusion) | non-fusion elementwise | flops 2097152 | bytes 12582912 | tf_op jit(solution)/shard_map/convert_element_type | solution.py:114
  350.6 7.0 %all-to-all-start.2 = ((bf16[16,512,256]{2,1,0:T(8,128)(2,1)}), bf16[16,512,256]{2,1,0:T(8,128)(2,1)}, u32[]{:S(2)}, u32[]{:S(2)}) async-start(bf16[16,512,256]{2,1,0:T(8,128)(2,1)} %convert_element_type.85), calls=%async_computation.2 | async-start | bytes 8388608 | tf_op jit(solution)/shard_map/all_to_all | solution.py:113
  357.7 3.2 fusion.92
  360.8 3.5 convolution_add_fusion.4
  366.5 4.7 %fusion.30 = f32[4,512,256]{2,0,1:T(4,128)S(1)} fusion(bf16[16,512,256]{2,1,0:T(8,128)(2,1)} %all-to-all-done.3, s32[16]{0:T(128)S(1)} %copy-done.36, pred[16]{0:T(512)(128)(4,1)S(1)} %copy-done.34), kind=kOutput, calls=%fused_computation.60 | convolution fusion | flops 16777344 | bytes 6291536 | tf_op jit(solution)/shard_map/ij,jrd->ird/dot_general | solution.py:124
  372.6 9.3 %collective-permute-start.3 = (bf16[2,512,256]{2,1,0:T(8,128)(2,1)}, bf16[2,512,256]{2,1,0:T(8,128)(2,1)}, u32[]{:S(2)}, u32[]{:S(2)}) collective-permute-start(bf16[2,512,256]{2,1,0:T(8,128)(2,1)} %copy.250), channel_id=1, source_target_pairs={{0,16},{16,32},{32,48},{48,64},{64,80},{80,96},{96,112},{112,0},{1... | collective-permute-start | bytes 1572872 | tf_op jit(solution)/shard_map/ppermute | solution.py:12
  381.9 29.4 %all-to-all-done.2 = bf16[16,512,256]{2,1,0:T(8,128)(2,1)} async-done(((bf16[16,512,256]{2,1,0:T(8,128)(2,1)}), bf16[16,512,256]{2,1,0:T(8,128)(2,1)}, u32[]{:S(2)}, u32[]{:S(2)}) %all-to-all-start.2) | async-done | bytes 4194336 | tf_op jit(solution)/shard_map/all_to_all | solution.py:113
  411.4 4.8 %fusion.32 = f32[4,512,256]{2,0,1:T(4,128)S(1)} fusion(bf16[16,512,256]{2,1,0:T(8,128)(2,1)} %all-to-all-done.2, s32[16]{0:T(128)S(1)} %copy-done.36, pred[16]{0:T(512)(128)(4,1)S(1)} %copy-done.34), kind=kOutput, calls=%fused_computation.62 | convolution fusion | flops 16777344 | bytes 6291536 | tf_op jit(solution)/shard_map/ij,jrd->ird/dot_general | solution.py:123
  417.7 15.6 %collective-permute-start.2 = (bf16[2,512,256]{2,1,0:T(8,128)(2,1)}, bf16[2,512,256]{2,1,0:T(8,128)(2,1)}, u32[]{:S(2)}, u32[]{:S(2)}) collective-permute-start(bf16[2,512,256]{2,1,0:T(8,128)(2,1)} %copy.251), channel_id=1, source_target_pairs={{0,16},{16,32},{32,48},{48,64},{64,80},{80,96},{96,112},{112,0},{1... | collective-permute-start | bytes 1572872 | tf_op jit(solution)/shard_map/ppermute | solution.py:12
  435.3 2.0 slice.122
  437.2 2.0 fusion.39
  439.8 2.0 fusion.40
  (178 shorter events, 48.8 us)
Async XLA Ops:
  0.6 15.3 %copy-start.31 = (bf16[1,1024,256]{2,1,0:T(8,128)(2,1)S(1)}, bf16[1,1024,256]{2,1,0:T(8,128)(2,1)}, u32[]{:S(2)}) copy-start(bf16[1,1024,256]{2,1,0:T(8,128)(2,1)} %param.11) | copy-start | bytes 1572868
  0.6 9.7 %collective-permute-start = (bf16[2,512,256]{2,1,0:T(8,128)(2,1)}, bf16[2,512,256]{2,1,0:T(8,128)(2,1)S(1)}, u32[]{:S(2)}, u32[]{:S(2)}) collective-permute-start(bf16[2,512,256]{2,1,0:T(8,128)(2,1)} %bitcast.348), channel_id=1, source_target_pairs={{0,112},{16,0},{32,16},{48,32},{64,48},{80,64},{96,80},{112,96},{1... | collective-permute-start | bytes 1572872 | tf_op jit(solution)/shard_map/ppermute | solution.py:12
  2.1 13.9 %collective-permute-start.1 = (bf16[2,512,256]{2,1,0:T(8,128)(2,1)}, bf16[2,512,256]{2,1,0:T(8,128)(2,1)S(1)}, u32[]{:S(2)}, u32[]{:S(2)}) collective-permute-start(bf16[2,512,256]{2,1,0:T(8,128)(2,1)} %bitcast.350), channel_id=1, source_target_pairs={{0,112},{16,0},{32,16},{48,32},{64,48},{80,64},{96,80},{112,96},{1... | collective-permute-start | bytes 1572872 | tf_op jit(solution)/shard_map/ppermute | solution.py:12
  6.5 12.4 %copy-start.35 = (s32[16]{0:T(128)}, s32[16]{0:T(128)S(1)}, u32[]{:S(2)}) copy-start(s32[16]{0:T(128)S(1)} %fusion.65) | copy-start | bytes 196
  25.1 62.2 %copy-start.32 = (bf16[512,256]{1,0:T(8,128)(2,1)S(1)}, bf16[512,256]{1,0:T(8,128)(2,1)}, u32[]{:S(2)}) copy-start(bf16[512,256]{1,0:T(8,128)(2,1)} %param.9) | copy-start | bytes 786436
  25.1 62.3 %copy-start.33 = (bf16[512,256]{1,0:T(8,128)(2,1)S(1)}, bf16[512,256]{1,0:T(8,128)(2,1)}, u32[]{:S(2)}) copy-start(bf16[512,256]{1,0:T(8,128)(2,1)} %param.12) | copy-start | bytes 786436
  82.5 63.5 %all-to-all-start.1 = ((bf16[16,512,256]{2,1,0:T(8,128)(2,1)}), bf16[16,512,256]{2,1,0:T(8,128)(2,1)}, u32[]{:S(2)}, u32[]{:S(2)}) async-start(bf16[16,512,256]{2,1,0:T(8,128)(2,1)} %get-tuple-element.40), calls=%async_computation.1 | async-start | bytes 8388608 | tf_op jit(solution)/shard_map/all_to_all | solution.py:66
  153.3 9.1 %copy-start.12 = (bf16[1,512,256]{1,2,0:T(8,128)(2,1)}, bf16[1,512,256]{1,2,0:T(8,128)(2,1)S(1)}, u32[]{:S(2)}) copy-start(bf16[1,512,256]{1,2,0:T(8,128)(2,1)S(1)} %copy.163) | copy-start | bytes 786436
  162.6 9.3 %copy-start.14 = (bf16[1,512,256]{1,2,0:T(8,128)(2,1)}, bf16[1,512,256]{1,2,0:T(8,128)(2,1)S(1)}, u32[]{:S(2)}) copy-start(bf16[1,512,256]{1,2,0:T(8,128)(2,1)S(1)} %copy.162) | copy-start | bytes 786436
  167.3 9.2 %copy-start.16 = (bf16[1,512,256]{1,2,0:T(8,128)(2,1)}, bf16[1,512,256]{1,2,0:T(8,128)(2,1)S(1)}, u32[]{:S(2)}) copy-start(bf16[1,512,256]{1,2,0:T(8,128)(2,1)S(1)} %copy.161) | copy-start | bytes 786436
  172.0 5.4 %copy-start.10 = (bf16[1,512,256]{1,2,0:T(8,128)(2,1)}, bf16[1,512,256]{1,2,0:T(8,128)(2,1)S(1)}, u32[]{:S(2)}) copy-start(bf16[1,512,256]{1,2,0:T(8,128)(2,1)S(1)} %copy.158) | copy-start | bytes 786436
  177.4 3.5 copy-start
  177.4 7.7 %slice-start.10 = ((s8[8388608]{0:T(1024)(128)(4,1)}), s8[4194304]{0:T(1024)(128)(4,1)S(1)}, s32[]{:S(2)}) async-start(s8[8388608]{0:T(1024)(128)(4,1)} %bitcast.274), calls=%async_computation.14 | async-start | bytes 8388608
  179.8 4.4 copy-start.1
  181.0 5.3 %slice-start.11 = ((s8[8388608]{0:T(1024)(128)(4,1)}), s8[4194304]{0:T(1024)(128)(4,1)S(1)}, s32[]{:S(2)}) async-start(s8[8388608]{0:T(1024)(128)(4,1)} %bitcast.274), calls=%async_computation.15 | async-start | bytes 8388608
  182.4 5.3 %slice-start.8 = ((s8[8388608]{0:T(1024)(128)(4,1)}), s8[4194304]{0:T(1024)(128)(4,1)S(1)}, s32[]{:S(2)}) async-start(s8[8388608]{0:T(1024)(128)(4,1)} %bitcast.272), calls=%async_computation.12 | async-start | bytes 8388608
  182.4 6.3 %slice-start.9 = ((s8[8388608]{0:T(1024)(128)(4,1)}), s8[4194304]{0:T(1024)(128)(4,1)S(1)}, s32[]{:S(2)}) async-start(s8[8388608]{0:T(1024)(128)(4,1)} %bitcast.272), calls=%async_computation.13 | async-start | bytes 8388608
  184.2 5.9 %slice-start.4 = ((s8[8388608]{0:T(1024)(128)(4,1)}), s8[4194304]{0:T(1024)(128)(4,1)S(1)}, s32[]{:S(2)}) async-start(s8[8388608]{0:T(1024)(128)(4,1)} %bitcast.268), calls=%async_computation.8 | async-start | bytes 8388608
  187.7 3.6 slice-start.5
  188.7 4.0 slice-start
  191.3 2.4 slice-start.1
  214.6 4.8 %copy-start.30 = (bf16[1,512,256]{2,1,0:T(8,128)(2,1)S(1)}, bf16[1,512,256]{2,1,0:T(8,128)(2,1)}, u32[]{:S(2)}) copy-start(bf16[1,512,256]{2,1,0:T(8,128)(2,1)} %get-tuple-element.31) | copy-start | bytes 786436
  217.1 7.4 %copy-start.29 = (bf16[1,512,256]{2,1,0:T(8,128)(2,1)S(1)}, bf16[1,512,256]{2,1,0:T(8,128)(2,1)}, u32[]{:S(2)}) copy-start(bf16[1,512,256]{2,1,0:T(8,128)(2,1)} %get-tuple-element.30) | copy-start | bytes 786436
  217.1 7.6 %copy-start.28 = (bf16[1,512,256]{2,1,0:T(8,128)(2,1)S(1)}, bf16[1,512,256]{2,1,0:T(8,128)(2,1)}, u32[]{:S(2)}) copy-start(bf16[1,512,256]{2,1,0:T(8,128)(2,1)} %get-tuple-element.29) | copy-start | bytes 786436
  217.1 7.7 %copy-start.27 = (bf16[1,512,256]{2,1,0:T(8,128)(2,1)S(1)}, bf16[1,512,256]{2,1,0:T(8,128)(2,1)}, u32[]{:S(2)}) copy-start(bf16[1,512,256]{2,1,0:T(8,128)(2,1)} %get-tuple-element.28) | copy-start | bytes 786436
  217.1 7.9 %copy-start.26 = (bf16[1,512,256]{2,1,0:T(8,128)(2,1)S(1)}, bf16[1,512,256]{2,1,0:T(8,128)(2,1)}, u32[]{:S(2)}) copy-start(bf16[1,512,256]{2,1,0:T(8,128)(2,1)} %get-tuple-element.27) | copy-start | bytes 786436
  217.1 8.0 %copy-start.25 = (bf16[1,512,256]{2,1,0:T(8,128)(2,1)S(1)}, bf16[1,512,256]{2,1,0:T(8,128)(2,1)}, u32[]{:S(2)}) copy-start(bf16[1,512,256]{2,1,0:T(8,128)(2,1)} %get-tuple-element.26) | copy-start | bytes 786436
  230.1 10.1 %slice-start.6 = ((s8[8388608]{0:T(1024)(128)(4,1)}), s8[4194304]{0:T(1024)(128)(4,1)S(1)}, s32[]{:S(2)}) async-start(s8[8388608]{0:T(1024)(128)(4,1)} %bitcast.270), calls=%async_computation.10 | async-start | bytes 8388608
  235.2 5.1 %slice-start.7 = ((s8[8388608]{0:T(1024)(128)(4,1)}), s8[4194304]{0:T(1024)(128)(4,1)S(1)}, s32[]{:S(2)}) async-start(s8[8388608]{0:T(1024)(128)(4,1)} %bitcast.270), calls=%async_computation.11 | async-start | bytes 8388608
  235.2 6.6 %slice-start.2 = ((s8[8388608]{0:T(1024)(128)(4,1)}), s8[4194304]{0:T(1024)(128)(4,1)S(1)}, s32[]{:S(2)}) async-start(s8[8388608]{0:T(1024)(128)(4,1)} %bitcast.266), calls=%async_computation.6 | async-start | bytes 8388608
  240.3 2.4 slice-start.3
  242.7 7.9 %slice-start.14 = ((s8[8388608]{0:T(1024)(128)(4,1)}), s8[4194304]{0:T(1024)(128)(4,1)S(1)}, s32[]{:S(2)}) async-start(s8[8388608]{0:T(1024)(128)(4,1)} %bitcast.278), calls=%async_computation.18 | async-start | bytes 8388608
  244.3 6.4 %slice-start.15 = ((s8[8388608]{0:T(1024)(128)(4,1)}), s8[4194304]{0:T(1024)(128)(4,1)S(1)}, s32[]{:S(2)}) async-start(s8[8388608]{0:T(1024)(128)(4,1)} %bitcast.278), calls=%async_computation.19 | async-start | bytes 8388608
  244.3 10.2 %slice-start.12 = ((s8[8388608]{0:T(1024)(128)(4,1)}), s8[4194304]{0:T(1024)(128)(4,1)S(1)}, s32[]{:S(2)}) async-start(s8[8388608]{0:T(1024)(128)(4,1)} %bitcast.276), calls=%async_computation.16 | async-start | bytes 8388608
  250.6 3.9 slice-start.13
  254.5 3.9 copy-start.24
  254.5 4.7 %copy-start.23 = (f32[8,512,32]{1,2,0:T(8,128)S(1)}, f32[8,512,32]{1,2,0:T(8,128)}, u32[]{:S(2)}) copy-start(f32[8,512,32]{1,2,0:T(8,128)} %fusion.53) | copy-start | bytes 1572868
  254.5 5.5 %copy-start.22 = (f32[8,512,32]{1,2,0:T(8,128)S(1)}, f32[8,512,32]{1,2,0:T(8,128)}, u32[]{:S(2)}) copy-start(f32[8,512,32]{1,2,0:T(8,128)} %fusion.50) | copy-start | bytes 1572868
  254.5 6.3 %copy-start.21 = (f32[8,512,32]{1,2,0:T(8,128)S(1)}, f32[8,512,32]{1,2,0:T(8,128)}, u32[]{:S(2)}) copy-start(f32[8,512,32]{1,2,0:T(8,128)} %fusion.47) | copy-start | bytes 1572868
  254.5 7.2 %copy-start.20 = (f32[8,512,32]{1,2,0:T(8,128)S(1)}, f32[8,512,32]{1,2,0:T(8,128)}, u32[]{:S(2)}) copy-start(f32[8,512,32]{1,2,0:T(8,128)} %fusion.44) | copy-start | bytes 1572868
  254.5 8.0 %copy-start.19 = (f32[8,512,32]{1,2,0:T(8,128)S(1)}, f32[8,512,32]{1,2,0:T(8,128)}, u32[]{:S(2)}) copy-start(f32[8,512,32]{1,2,0:T(8,128)} %fusion.41) | copy-start | bytes 1572868
  284.1 66.5 %all-to-all-start.3 = ((bf16[16,512,256]{2,1,0:T(8,128)(2,1)}), bf16[16,512,256]{2,1,0:T(8,128)(2,1)}, u32[]{:S(2)}, u32[]{:S(2)}) async-start(bf16[16,512,256]{2,1,0:T(8,128)(2,1)} %convert_element_type.88), calls=%async_computation.3 | async-start | bytes 8388608 | tf_op jit(solution)/shard_map/all_to_all | solution.py:116
  306.9 2.0 copy-start.5
  315.8 2.0 copy-start.7
  324.9 2.0 copy-start.2
  344.7 12.9 %copy-start.11 = (bf16[1,512,256]{1,2,0:T(8,128)(2,1)S(1)}, bf16[1,512,256]{1,2,0:T(8,128)(2,1)}, u32[]{:S(2)}) copy-start(bf16[1,512,256]{1,2,0:T(8,128)(2,1)} %copy-done.10) | copy-start | bytes 786436
  350.6 10.2 %copy-start.18 = (bf16[1,512,256]{1,2,0:T(8,128)(2,1)S(1)}, bf16[1,512,256]{1,2,0:T(8,128)(2,1)}, u32[]{:S(2)}) copy-start(bf16[1,512,256]{1,2,0:T(8,128)(2,1)} %copy.160) | copy-start | bytes 786436
  350.6 13.7 %copy-start.17 = (bf16[1,512,256]{1,2,0:T(8,128)(2,1)S(1)}, bf16[1,512,256]{1,2,0:T(8,128)(2,1)}, u32[]{:S(2)}) copy-start(bf16[1,512,256]{1,2,0:T(8,128)(2,1)} %copy-done.16) | copy-start | bytes 786436
  350.6 60.7 %all-to-all-start.2 = ((bf16[16,512,256]{2,1,0:T(8,128)(2,1)}), bf16[16,512,256]{2,1,0:T(8,128)(2,1)}, u32[]{:S(2)}, u32[]{:S(2)}) async-start(bf16[16,512,256]{2,1,0:T(8,128)(2,1)} %convert_element_type.85), calls=%async_computation.2 | async-start | bytes 8388608 | tf_op jit(solution)/shard_map/all_to_all | solution.py:113
  357.6 6.7 %copy-start.4 = (bf16[8,512,512]{1,2,0:T(8,128)(2,1)S(1)}, bf16[8,512,512]{1,2,0:T(8,128)(2,1)}, u32[]{:S(2)}) copy-start(bf16[8,512,512]{1,2,0:T(8,128)(2,1)} %fusion.3) | copy-start | bytes 12582916
  357.6 7.4 %copy-start.6 = (bf16[8,512,512]{1,2,0:T(8,128)(2,1)S(1)}, bf16[8,512,512]{1,2,0:T(8,128)(2,1)}, u32[]{:S(2)}) copy-start(bf16[8,512,512]{1,2,0:T(8,128)(2,1)} %copy-done.5) | copy-start | bytes 12582916
  357.6 7.4 %copy-start.15 = (bf16[1,512,256]{1,2,0:T(8,128)(2,1)S(1)}, bf16[1,512,256]{1,2,0:T(8,128)(2,1)}, u32[]{:S(2)}) copy-start(bf16[1,512,256]{1,2,0:T(8,128)(2,1)} %copy-done.14) | copy-start | bytes 786436
  360.8 5.0 %copy-start.8 = (bf16[8,512,512]{1,2,0:T(8,128)(2,1)S(1)}, bf16[8,512,512]{1,2,0:T(8,128)(2,1)}, u32[]{:S(2)}) copy-start(bf16[8,512,512]{1,2,0:T(8,128)(2,1)} %copy-done.7) | copy-start | bytes 12582916
  360.8 5.0 %copy-start.13 = (bf16[1,512,256]{1,2,0:T(8,128)(2,1)S(1)}, bf16[1,512,256]{1,2,0:T(8,128)(2,1)}, u32[]{:S(2)}) copy-start(bf16[1,512,256]{1,2,0:T(8,128)(2,1)} %copy-done.12) | copy-start | bytes 786436
  364.3 2.2 copy-start.34
  364.3 2.2 copy-start.36
  372.6 64.6 %collective-permute-start.3 = (bf16[2,512,256]{2,1,0:T(8,128)(2,1)}, bf16[2,512,256]{2,1,0:T(8,128)(2,1)}, u32[]{:S(2)}, u32[]{:S(2)}) collective-permute-start(bf16[2,512,256]{2,1,0:T(8,128)(2,1)} %copy.250), channel_id=1, source_target_pairs={{0,16},{16,32},{32,48},{48,64},{64,80},{80,96},{96,112},{112,0},{1... | collective-permute-start | bytes 1572872 | tf_op jit(solution)/shard_map/ppermute | solution.py:12
  411.4 22.0 %copy-start.3 = (bf16[8,512,512]{1,2,0:T(8,128)(2,1)S(1)}, bf16[8,512,512]{1,2,0:T(8,128)(2,1)}, u32[]{:S(2)}) copy-start(bf16[8,512,512]{1,2,0:T(8,128)(2,1)} %copy-done.2) | copy-start | bytes 12582916
  416.2 17.9 %copy-start.9 = (f32[4,512,256]{2,0,1:T(4,128)}, f32[4,512,256]{2,0,1:T(4,128)S(1)}, u32[]{:S(2)}) copy-start(f32[4,512,256]{2,0,1:T(4,128)S(1)} %fusion.32) | copy-start | bytes 6291460
  417.7 22.1 %collective-permute-start.2 = (bf16[2,512,256]{2,1,0:T(8,128)(2,1)}, bf16[2,512,256]{2,1,0:T(8,128)(2,1)}, u32[]{:S(2)}, u32[]{:S(2)}) collective-permute-start(bf16[2,512,256]{2,1,0:T(8,128)(2,1)} %copy.251), channel_id=1, source_target_pairs={{0,16},{16,32},{32,48},{48,64},{64,80},{80,96},{96,112},{112,0},{1... | collective-permute-start | bytes 1572872 | tf_op jit(solution)/shard_map/ppermute | solution.py:12
where the time goes:
time: 450 us; the launch traced here: 442 us
  matrix products  134 us (30%)
  waiting for transfers between devices  90.9 us (20%)
  local copies, waits for them, and re-layouts  77.4 us (17%)
  blocking collectives  57.4 us (13%)
  starting transfers between devices  45 us (10%)
  other arithmetic  35.9 us (8%)
    all_to_all x1, blocking collectives, local(): lax.all_to_all(send_keys, 'band', split_axis=0, concat_axis=0, tiled=True)  57.4 us
    all_to_all x1, waiting for transfers between devices, local(): lax.all_to_all(send_values, 'band', split_axis=0, concat_axis=0, tiled=True)  55.4 us
    all_to_all x1, waiting for transfers between devices, local(): lax.all_to_all(slot_keys.astype(jnp.bfloat16), 'band', split_axis=0, conc...  29.4 us
    ppermute x4, starting transfers between devices, from_behind(): lax.ppermute(x, axis, [(i, (i + by) % length) for i in range(length)])  28.7 us
    dot_general x6, matrix products, block_terms(): jnp.einsum('qhd,khd->hqk', grads, block_values, preferred_element_type=jn...  28 us
    dot_general x6, matrix products, block_scores(): jnp.einsum('qhd,khd->hqk', queries, block_keys, preferred_element_type=jn...  25.2 us
    unnamed x121, local copies, waits for them, and re-layouts  24.6 us
    dot_general x6, matrix products, key_value_grads(): jnp.einsum('hqk,qhd->khd', probs_low, grads, preferred_element_type=jnp.f...  24.2 us
  transfers between devices with their start and end apart: 7, of which 5 were waited for; matrix products, arithmetic and copies ran while one was open for 21% of the time, Pallas kernels for 0%

commit v1 on v0

v1 whole, which is shorter than its diff:
```python
import functools

import jax
import jax.numpy as jnp
from jax import lax
from jax.experimental import pallas as pl
from jax.experimental.pallas import tpu as pltpu
from jax.sharding import PartitionSpec as P

HEADS = 8
BLOCK = 512
VIS = 6
HEAD_DIM = 32
TILES = 8
SCALE = HEAD_DIM**-0.5
LOG2E = 1.4426950408889634
ROWS = 256
bf16 = jnp.bfloat16
f32 = jnp.float32


def dot(a, b, contract_a, contract_b):
    return lax.dot_general(
        a, b, (((contract_a,), (contract_b,)), ((), ())), preferred_element_type=f32
    )


def two_parts(x):
    high = x.astype(bf16)
    return jnp.concatenate([high, (x - high.astype(f32)).astype(bf16)], axis=0)


def fold(x):
    return functools.reduce(jnp.add, [x[:, i : i + 128] for i in range(0, x.shape[1], 128)])


def fold_max(x):
    return functools.reduce(jnp.maximum, [x[:, i : i + 128] for i in range(0, x.shape[1], 128)])


def head_kernel(ids, kt, vt, qt, gt, dqt, dkt, dvt, s_ref, e_ref, dp_ref, ds_ref):
    dkt[...] = jnp.zeros_like(dkt)
    dvt[...] = jnp.zeros_like(dvt)

    def tile(t, _):
        q_t, g_t = qt[t], gt[t]
        q = q_t.astype(f32).T.astype(bf16)
        g = g_t.astype(f32).T.astype(bf16)
        for r in range(0, BLOCK, ROWS):
            rows = slice(r, r + ROWS)
            top = None
            for j in range(VIS):
                s = dot(q[rows], kt[ids[t, j]], 1, 0)
                s_ref[:, j * BLOCK : (j + 1) * BLOCK] = s
                part = fold_max(s)
                top = part if top is None else jnp.maximum(top, part)
            top = jnp.max(top, axis=1, keepdims=True) * (SCALE * LOG2E)
            total = weighted = None
            for j in range(VIS):
                cols = slice(j * BLOCK, (j + 1) * BLOCK)
                e = jnp.exp2(s_ref[:, cols] * (SCALE * LOG2E) - top)
                dp = dot(g[rows], vt[ids[t, j]], 1, 0)
                low = e.astype(bf16)
                e_ref[:, cols] = low
                dp_ref[:, cols] = dp
                e_part, w_part = fold(e), fold(low.astype(f32) * dp)
                total = e_part if total is None else total + e_part
                weighted = w_part if weighted is None else weighted + w_part
            inverse = 1.0 / jnp.sum(total, axis=1, keepdims=True)
            delta = jnp.sum(weighted, axis=1, keepdims=True) * inverse
            across = jnp.broadcast_to(inverse, (ROWS, 128)).T[:1]
            qq = two_parts(q_t[:, rows].astype(f32) * across)
            gg = two_parts(g_t[:, rows].astype(f32) * across)
            for j in range(VIS):
                cols = slice(j * BLOCK, (j + 1) * BLOCK)
                low = e_ref[:, cols]
                ds = (low.astype(f32) * (dp_ref[:, cols] - delta)).astype(bf16)
                ds_ref[:, cols] = ds
                block = ids[t, j]
                part = dot(gg, low, 1, 0)
                dvt[block] += part[:HEAD_DIM] + part[HEAD_DIM:]
                part = dot(qq, ds, 1, 0)
                dkt[block] += (part[:HEAD_DIM] + part[HEAD_DIM:]) * SCALE
            keys = jnp.concatenate([kt[ids[t, j]] for j in range(VIS)], axis=1)
            dq = dot(ds_ref[...], keys, 1, 1)
            dqt[t, :, rows] = (dq * (inverse * SCALE)).T.astype(bf16)
        return None

    lax.fori_loop(0, TILES, tile, None)


def head_grads(ids, kt, vt, qt, gt):
    vmem = pl.BlockSpec(memory_space=pltpu.VMEM)
    wide = VIS * BLOCK
    return pl.pallas_call(
        head_kernel,
        out_shape=[
            jax.ShapeDtypeStruct(qt.shape, bf16),
            jax.ShapeDtypeStruct(kt.shape, f32),
            jax.ShapeDtypeStruct(kt.shape, f32),
        ],
        in_specs=[pl.BlockSpec(memory_space=pltpu.SMEM)] + [vmem] * 4,
        out_specs=[vmem] * 3,
        scratch_shapes=[
            pltpu.VMEM((ROWS, wide), f32),
            pltpu.VMEM((ROWS, wide), bf16),
            pltpu.VMEM((ROWS, wide), f32),
            pltpu.VMEM((ROWS, wide), bf16),
        ],
        compiler_params=pltpu.CompilerParams(vmem_limit_bytes=56 << 20),
    )(ids, kt, vt, qt, gt)


def shift_cam(x, by):
    length = lax.axis_size("cam")
    return lax.ppermute(x, "cam", [(i, (i + by) % length) for i in range(length)])


def local(query, key_img, value_img, d_out, visible):
    cams, bands = lax.axis_size("cam"), lax.axis_size("band")
    cam, band = lax.axis_index("cam"), lax.axis_index("band")
    halves = [[h * HEADS + i for i in range(HEADS)] for h in range(bands // HEADS)]

    def by_head(x):
        return x.reshape(-1, BLOCK, HEADS, HEAD_DIM).transpose(2, 0, 3, 1)

    pairs = jnp.stack([by_head(key_img), by_head(value_img)], axis=1)
    pairs = jnp.concatenate([pairs] * (bands // HEADS), axis=0)
    own = lax.all_to_all(pairs, "band", 0, 0, tiled=True)
    following = shift_cam(own, -1)
    both = jnp.concatenate([own, following], axis=0)
    kt = both[:, 0].reshape(-1, HEAD_DIM, BLOCK)
    vt = both[:, 1].reshape(-1, HEAD_DIM, BLOCK)
    tiles = jnp.stack([by_head(query)[:, 0], by_head(d_out)[:, 0]], axis=1)
    tiles = lax.all_to_all(tiles, "band", 0, 0, tiled=True, axis_index_groups=halves)
    start = cam * bands + band // HEADS * TILES
    ids = lax.dynamic_slice_in_dim(visible, start, TILES, 0)
    per_cam = 2 * bands
    ids = (ids // per_cam - cam) % cams * per_cam + ids % per_cam
    dqt, dkt, dvt = head_grads(ids, kt, vt, tiles[:, 0], tiles[:, 1])
    grads = jnp.stack(
        [x.reshape(2, bands, 2, HEAD_DIM, BLOCK) for x in (dkt, dvt)], axis=2
    )
    came = shift_cam(grads[1].astype(bf16), 1)
    grads = (grads[0] + came.astype(f32)).astype(bf16)
    back = lax.all_to_all(grads, "band", 0, 0, tiled=True)
    back = back.reshape(bands // HEADS, HEADS, 2, 2, HEAD_DIM, BLOCK)
    back = jnp.sum(back.astype(f32), axis=0).astype(bf16)
    back = back.transpose(1, 2, 4, 0, 3).reshape(2, 1, 2 * BLOCK, HEADS * HEAD_DIM)
    dqt = lax.all_to_all(dqt, "band", 0, 0, tiled=True, axis_index_groups=halves)
    d_query = dqt.transpose(2, 0, 1).reshape(BLOCK, HEADS * HEAD_DIM)
    return d_query, back[0], back[1]


def solution(mesh):
    in_specs = (
        P(("cam", "band"), None),
        P("cam", "band", None),
        P("cam", "band", None),
        P(("cam", "band"), None),
        P(),
    )
    out_specs = (P(("cam", "band"), None), P("cam", "band", None), P("cam", "band", None))
    return jax.shard_map(local, mesh=mesh, in_specs=in_specs, out_specs=out_specs, check_vma=False)
```

time: 450 us -> 208 us (0.46)
  the two profiles are of different devices: /device:TPU:1 before, /device:TPU:2 now
where the time goes in v1:
time: 208 us; the launch traced here: 207 us
  waiting for transfers between devices  65.4 us (31%)
  Pallas kernels  55.2 us (27%)
  blocking collectives  36.4 us (18%)
  local copies, waits for them, and re-layouts  23.6 us (11%)
  other arithmetic  13 us (6%)
  starting transfers between devices  12.9 us (6%)
    pallas_call x1, Pallas kernels, head_grads(): pl.pallas_call(head_kernel, out_shape=[jax.ShapeDtypeStruct(qt.shape, bf1...  55.2 us
    all_to_all x1, blocking collectives, local(): own = lax.all_to_all(pairs, 'band', 0, 0, tiled=True)  36.4 us
    all_to_all x1, waiting for transfers between devices, local(): back = lax.all_to_all(grads, 'band', 0, 0, tiled=True)  29.4 us
    ppermute x2, waiting for transfers between devices, shift_cam(): lax.ppermute(x, 'cam', [(i, (i + by) % length) for i in range(length)])  25.9 us
    all_to_all x1, waiting for transfers between devices, local(): lax.all_to_all(tiles, 'band', 0, 0, tiled=True, axis_index_groups=halves)  9.99 us
    unnamed x18, local copies, waits for them, and re-layouts  6.53 us
    convert_element_type x1, other arithmetic, local(): grads = (grads[0] + came.astype(f32)).astype(bf16)  5.03 us
    slice x2, local copies, waits for them, and re-layouts, local(): vt = both[:, 1].reshape(-1, HEAD_DIM, BLOCK)  4.98 us
  transfers between devices with their start and end apart: 5, of which 4 were waited for; matrix products, arithmetic and copies ran while one was open for 5% of the time, Pallas kernels for 0%

profile of v1, /device:TPU:2, one launch (start us, length us, event | category | flops | bytes accessed | tf_op | source)
XLA Modules:
  0.0 207.3 jit_solution(6638939341768282939)
XLA Ops:
  0.6 0.0 copy-start
  0.6 0.0 copy-start.1
  0.7 1.3 copy.27
  2.0 0.4 reshape.30
  2.3 0.0 copy-done.1
  2.4 0.2 copy.28
  2.6 0.4 reshape.31
  2.9 3.4 %maximum_maximum_fusion = bf16[16,2,2,32,512]{4,2,3,0,1:T(2,128)(2,1)S(1)} fusion(bf16[8,1,2,32,512]{4,2,3,0,1:T(2,128)(2,1)S(1)} %bitcast.60, bf16[8,1,2,32,512]{4,2,3,0,1:T(2,128)(2,1)S(1)} %bitcast.59), kind=kLoop, calls=%fused_computation.9 | loop fusion | flops 3145728 | bytes 3145728 | tf_op jit(solution)/shard_map/concatenate | solution.py:128
  6.4 2.5 %copy.29 = bf16[16,2,2,32,512]{4,2,3,1,0:T(2,128)(2,1)S(1)} copy(bf16[16,2,2,32,512]{4,2,3,0,1:T(2,128)(2,1)S(1)} %maximum_maximum_fusion) | data formatting | bytes 4194304 | tf_op jit(solution)/shard_map/concatenate | solution.py:128
  8.9 0.0 copy-start.2
  8.9 0.0 copy-start.3
  8.9 36.4 %all_to_all.20 = bf16[16,2,2,32,512]{4,2,3,1,0:T(2,128)(2,1)S(1)} all-to-all(bf16[16,2,2,32,512]{4,2,3,1,0:T(2,128)(2,1)S(1)} %copy.29), channel_id=1, replica_groups=mesh['cam'=8,'band'=16] {'band'}, dimensions={0} | all-to-all | bytes 4194304 | tf_op jit(solution)/shard_map/all_to_all | solution.py:129
  45.3 0.0 collective-permute-start
  45.3 0.0 copy-done.2
  45.3 0.1 copy.32
  45.4 0.0 copy-done.3
  45.4 0.1 copy.33
  45.6 0.8 pad_maximum_fusion.1
  46.4 3.7 %all-to-all-start.1 = ((bf16[8,2,32,512]{3,2,1,0:T(8,128)(2,1)}), bf16[8,2,32,512]{3,2,1,0:T(8,128)(2,1)S(1)}, u32[]{:S(2)}, u32[]{:S(2)}) async-start(bf16[8,2,32,512]{3,2,1,0:T(8,128)(2,1)} %pad_maximum_fusion.1), calls=%async_computation.1 | async-start | bytes 1048576 | tf_op jit(solution)/shard_map/all_to_all | solution.py:135
  50.1 0.0 copy-done
  50.1 0.1 constant_dynamic-slice_fusion
  50.2 0.1 copy.45
  50.3 0.6 fusion.9.ids
  50.9 10.0 %all-to-all-done.1 = bf16[8,2,32,512]{3,2,1,0:T(8,128)(2,1)S(1)} async-done(((bf16[8,2,32,512]{3,2,1,0:T(8,128)(2,1)}), bf16[8,2,32,512]{3,2,1,0:T(8,128)(2,1)S(1)}, u32[]{:S(2)}, u32[]{:S(2)}) %all-to-all-start.1) | async-done | bytes 524320 | tf_op jit(solution)/shard_map/all_to_all | solution.py:135
  60.9 0.8 slice_bitcast_fusion
  61.7 1.7 constant_dynamic-update-slice_fusion.1
  63.4 5.4 %collective-permute-done = bf16[16,2,2,32,512]{4,2,3,1,0:T(2,128)(2,1)} collective-permute-done((bf16[16,2,2,32,512]{4,2,3,1,0:T(2,128)(2,1)S(1)}, bf16[16,2,2,32,512]{4,2,3,1,0:T(2,128)(2,1)}, u32[]{:S(2)}, u32[]{:S(2)}) %collective-permute-start) | collective-permute-done | bytes 2097184 | tf_op jit(solution)/shard_map/ppermute | solution.py:116
  68.8 4.2 %constant_dynamic-update-slice_fusion = bf16[32,2,2,32,512]{4,2,3,1,0:T(2,128)(2,1)S(1)} fusion(bf16[32,2,2,32,512]{4,2,3,1,0:T(2,128)(2,1)S(1)} %constant_dynamic-update-slice_fusion.1, bf16[16,2,2,32,512]{4,2,3,1,0:T(2,128)(2,1)} %collective-permute-done), kind=kLoop, calls=%fused_computation.14 | loop fusion | bytes 4194304 | tf_op jit(solution)/shard_map/concatenate | solution.py:131
  73.0 3.1 %fusion.11 = (bf16[32,1,2,32,512]{4,2,3,1,0:T(2,128)(2,1)S(1)}, bf16[32,1,2,32,512]{4,2,3,1,0:T(2,128)(2,1)S(1)}) fusion(bf16[32,2,2,32,512]{4,2,3,1,0:T(2,128)(2,1)S(1)} %constant_dynamic-update-slice_fusion), kind=kLoop, calls=%fused_computation.31 | loop fusion | bytes 8388608 | tf_op jit(solution)/shard_map/slice | solution.py:133
  76.2 1.8 copy.31
  78.0 1.9 copy.30
  79.9 55.2 %shard_map.76 = (bf16[8,32,512]{2,1,0:T(8,128)(2,1)}, f32[64,32,512]{2,1,0:T(8,128)}, f32[64,32,512]{2,1,0:T(8,128)}) custom-call(s32[8,6]{1,0:T(8,128)} %fusion.9.ids, bf16[64,32,512]{2,1,0:T(8,128)(2,1)} %bitcast.57, bf16[64,32,512]{2,1,0:T(8,128)(2,1)} %bitcast.56, bf16[8,32,512]{2,1,0:T(8,128)(2,1)} %get-tuple-element.23.qt, ...), custom_call_target="tpu_custom_call" | custom-call | tf_op jit(solution)/shard_map/pallas_call | solution.py:95
  135.0 2.5 %fusion.5 = bf16[16,2,2,32,512]{4,3,2,1,0:T(8,128)(2,1)S(1)} fusion(f32[2,16,1,2,32,512]{5,4,3,2,1,0:T(8,128)} %bitcast.53, f32[2,16,1,2,32,512]{5,4,3,2,1,0:T(8,128)} %bitcast.51), kind=kLoop, calls=%fused_computation.8 | loop fusion | flops 1048576 | bytes 10485760 | tf_op jit(solution)/shard_map/convert_element_type | solution.py:144
  137.5 1.9 collective-permute-start.1
  139.4 3.4 %all-to-all-start.2 = ((bf16[8,32,512]{2,1,0:T(8,128)(2,1)}), bf16[8,32,512]{2,1,0:T(8,128)(2,1)S(1)}, u32[]{:S(2)}, u32[]{:S(2)}) async-start(bf16[8,32,512]{2,1,0:T(8,128)(2,1)} %get-tuple-element.6), calls=%async_computation.2 | async-start | bytes 524288 | tf_op jit(solution)/shard_map/all_to_all | solution.py:150
  142.8 20.5 %collective-permute-done.1 = bf16[16,2,2,32,512]{4,3,2,1,0:T(8,128)(2,1)} collective-permute-done((bf16[16,2,2,32,512]{4,3,2,1,0:T(8,128)(2,1)S(1)}, bf16[16,2,2,32,512]{4,3,2,1,0:T(8,128)(2,1)}, u32[]{:S(2)}, u32[]{:S(2)}) %collective-permute-start.1) | collective-permute-done | bytes 2097184 | tf_op jit(solution)/shard_map/ppermute | solution.py:116
  163.3 5.0 %fusion.3 = bf16[16,2,2,32,512]{4,3,2,1,0:T(8,128)(2,1)} fusion(f32[2,16,1,2,32,512]{5,4,3,2,1,0:T(8,128)} %bitcast.52, f32[2,16,1,2,32,512]{5,4,3,2,1,0:T(8,128)} %bitcast.54, bf16[16,2,2,32,512]{4,3,2,1,0:T(8,128)(2,1)} %collective-permute-done.1), kind=kLoop, calls=%fused_computation.5 | loop fusion | flops 4194304 | bytes 12582912 | tf_op jit(solution)/shard_map/convert_element_type | solution.py:145
  168.4 0.0 all-to-all-done.2
  168.4 3.9 %all-to-all-start.3 = ((bf16[16,2,2,32,512]{4,3,2,1,0:T(8,128)(2,1)}), bf16[16,2,2,32,512]{4,3,2,1,0:T(8,128)(2,1)S(1)}, u32[]{:S(2)}, u32[]{:S(2)}) async-start(bf16[16,2,2,32,512]{4,3,2,1,0:T(8,128)(2,1)} %fusion.3), calls=%async_computation.3 | async-start | bytes 4194304 | tf_op jit(solution)/shard_map/all_to_all | solution.py:146
  172.3 0.8 copy.41
  173.2 29.4 %all-to-all-done.3 = bf16[16,2,2,32,512]{4,3,2,1,0:T(8,128)(2,1)S(1)} async-done(((bf16[16,2,2,32,512]{4,3,2,1,0:T(8,128)(2,1)}), bf16[16,2,2,32,512]{4,3,2,1,0:T(8,128)(2,1)S(1)}, u32[]{:S(2)}, u32[]{:S(2)}) %all-to-all-start.3) | async-done | bytes 2097184 | tf_op jit(solution)/shard_map/all_to_all | solution.py:146
  202.6 0.6 reduce_sum.12
  203.2 0.1 copy.49
  203.4 0.1 fusion.12
  203.5 0.5 copy.40
  204.0 0.4 squeeze.20
  204.4 1.0 copy.43
  205.4 0.5 copy.39
  205.9 0.4 squeeze.19
  206.3 1.0 copy.42
Async XLA Ops:
  0.6 49.5 %copy-start = (s32[128,6]{0,1:T(8,128)S(1)}, s32[128,6]{0,1:T(8,128)}, u32[]{:S(2)}) copy-start(s32[128,6]{0,1:T(8,128)} %param.9) | copy-start | bytes 9220
  0.6 1.7 copy-start.1
  8.9 36.4 %copy-start.2 = (bf16[512,256]{1,0:T(8,128)(2,1)S(1)}, bf16[512,256]{1,0:T(8,128)(2,1)}, u32[]{:S(2)}) copy-start(bf16[512,256]{1,0:T(8,128)(2,1)} %param.5) | copy-start | bytes 786436
  8.9 36.5 %copy-start.3 = (bf16[512,256]{1,0:T(8,128)(2,1)S(1)}, bf16[512,256]{1,0:T(8,128)(2,1)}, u32[]{:S(2)}) copy-start(bf16[512,256]{1,0:T(8,128)(2,1)} %param.8) | copy-start | bytes 786436
  45.3 23.6 %collective-permute-start = (bf16[16,2,2,32,512]{4,2,3,1,0:T(2,128)(2,1)S(1)}, bf16[16,2,2,32,512]{4,2,3,1,0:T(2,128)(2,1)}, u32[]{:S(2)}, u32[]{:S(2)}) collective-permute-start(bf16[16,2,2,32,512]{4,2,3,1,0:T(2,128)(2,1)S(1)} %all_to_all.20), channel_id=1, source_target_pairs={{0,112},{16,0},{32,16},{48,32},{64,48},{80,64},{96,80},{112,96},{1... | collective-permute-start | bytes 6291464 | tf_op jit(solution)/shard_map/ppermute | solution.py:116
  46.4 14.5 %all-to-all-start.1 = ((bf16[8,2,32,512]{3,2,1,0:T(8,128)(2,1)}), bf16[8,2,32,512]{3,2,1,0:T(8,128)(2,1)S(1)}, u32[]{:S(2)}, u32[]{:S(2)}) async-start(bf16[8,2,32,512]{3,2,1,0:T(8,128)(2,1)} %pad_maximum_fusion.1), calls=%async_computation.1 | async-start | bytes 1048576 | tf_op jit(solution)/shard_map/all_to_all | solution.py:135
  137.5 25.8 %collective-permute-start.1 = (bf16[16,2,2,32,512]{4,3,2,1,0:T(8,128)(2,1)S(1)}, bf16[16,2,2,32,512]{4,3,2,1,0:T(8,128)(2,1)}, u32[]{:S(2)}, u32[]{:S(2)}) collective-permute-start(bf16[16,2,2,32,512]{4,3,2,1,0:T(8,128)(2,1)S(1)} %fusion.5), channel_id=1, source_target_pairs={{0,16},{16,32},{32,48},{48,64},{64,80},{80,96},{96,112},{112,0},{1... | collective-permute-start | bytes 6291464 | tf_op jit(solution)/shard_map/ppermute | solution.py:116
  139.4 29.0 %all-to-all-start.2 = ((bf16[8,32,512]{2,1,0:T(8,128)(2,1)}), bf16[8,32,512]{2,1,0:T(8,128)(2,1)S(1)}, u32[]{:S(2)}, u32[]{:S(2)}) async-start(bf16[8,32,512]{2,1,0:T(8,128)(2,1)} %get-tuple-element.6), calls=%async_computation.2 | async-start | bytes 524288 | tf_op jit(solution)/shard_map/all_to_all | solution.py:150
  168.4 34.2 %all-to-all-start.3 = ((bf16[16,2,2,32,512]{4,3,2,1,0:T(8,128)(2,1)}), bf16[16,2,2,32,512]{4,3,2,1,0:T(8,128)(2,1)S(1)}, u32[]{:S(2)}, u32[]{:S(2)}) async-start(bf16[16,2,2,32,512]{4,3,2,1,0:T(8,128)(2,1)} %fusion.3), calls=%async_computation.3 | async-start | bytes 4194304 | tf_op jit(solution)/shard_map/all_to_all | solution.py:146

commit v2 on v1

v2 whole, which is shorter than its diff:
```python
import functools

import jax
import jax.numpy as jnp
from jax import lax
from jax.experimental import pallas as pl
from jax.experimental.pallas import tpu as pltpu
from jax.sharding import PartitionSpec as P

HEADS = 8
BLOCK = 512
VIS = 6
HEAD_DIM = 32
TILES = 8
BANDS = 16
CAMS = 8
BLOCKS = 2 * BANDS
WIDE = VIS * BLOCK
SCALE = HEAD_DIM**-0.5
LOG2E = 1.4426950408889634
COLS = [slice(j * BLOCK, (j + 1) * BLOCK) for j in range(VIS)]
bf16 = jnp.bfloat16
f32 = jnp.float32


def dot(a, b, contract_a, contract_b):
    return lax.dot_general(
        a, b, (((contract_a,), (contract_b,)), ((), ())), preferred_element_type=f32
    )


def two_parts(x):
    high = x.astype(bf16)
    return jnp.concatenate([high, (x - high.astype(f32)).astype(bf16)], axis=0)


def fold(x, op=jnp.add):
    return functools.reduce(op, [x[:, i : i + 128] for i in range(0, x.shape[1], 128)])


def as_row(x):
    return jnp.broadcast_to(x, (x.shape[0], 128)).T[:1]


def flip(x):
    return x.astype(f32).T.astype(bf16)


def join(old, new, op):
    return new if old is None else op(old, new)


def run_stages(*stages):
    for j in range(VIS):
        for step, _ in stages:
            step(j)
    for _, finish in stages:
        finish()


def loop(low, high, body):
    def step(i, _):
        body(i)
        return None

    lax.fori_loop(low, high, step, None)


def kernel(
    ids, slots, picks, query, key, value, grad,
    d_query, d_key, d_value,
    k_out, v_out, q_out, g_out,
    kt, vt, qt, gt,
    e, s, top, delta, inverse, parts, own,
    n_out, b_out, vn_in, vb_in, kn_in, kb_in,
    dq_out, dq_in,
    k_ss, k_rs, kf_ss, kf_rs, v_ss, v_rs, vf_ss, vf_rs,
    q_ss, q_rs, g_ss, g_rs,
    vn_ss, vn_rs, vb_ss, vb_rs, kn_ss, kn_rs, kb_ss, kb_rs, dq_ss, dq_rs,
):
    cam, band = lax.axis_index("cam"), lax.axis_index("band")
    before = lax.rem(cam + CAMS - 1, CAMS)
    after = lax.rem(cam + 1, CAMS)
    head = lax.rem(band, HEADS)
    first = band - head

    def copy(src, dst, send, recv, **where):
        return pltpu.make_async_remote_copy(
            src_ref=src, dst_ref=dst, send_sem=send, recv_sem=recv,
            device_id=where, device_id_type=pl.DeviceIdType.MESH,
        )

    def ahead(d):
        return lax.rem(band + d, BANDS)

    def behind(d):
        return lax.rem(band + BANDS - d, BANDS)

    barrier = pltpu.get_barrier_semaphore()

    def greet(d):
        pl.semaphore_signal(
            barrier, inc=1, device_id={"band": ahead(d)}, device_id_type=pl.DeviceIdType.MESH
        )

    loop(1, BANDS, greet)
    for other in (before, after):
        pl.semaphore_signal(
            barrier, inc=1, device_id={"cam": other}, device_id_type=pl.DeviceIdType.MESH
        )

    def spread(x, out, held):
        for i in range(2):
            out[:, i] = flip(x[i * BLOCK : (i + 1) * BLOCK]).reshape(HEADS, HEAD_DIM, BLOCK)
        held[pl.ds(2 * band, 2)] = out[head]

    def spread_copy(d, out, held, ss, rs):
        to = ahead(d)
        return copy(
            out.at[lax.rem(to, HEADS)], held.at[pl.ds(2 * band, 2)], ss.at[d], rs.at[band], band=to
        )

    def arrival(d, out, held, ss, rs):
        src = behind(d)
        return copy(out.at[0], held.at[pl.ds(2 * src, 2)], ss.at[d], rs.at[src], band=ahead(d))

    def forward(src, held, ss, rs):
        return copy(
            held.at[pl.ds(2 * src, 2)], held.at[pl.ds(BLOCKS + 2 * src, 2)],
            ss.at[src], rs.at[src], cam=before,
        )

    def relay(d, out, held, ss, rs, fss, frs):
        arrival(d, out, held, ss, rs).wait_recv()
        forward(behind(d), held, fss, frs).start()

    def share(x, out, held):
        out[...] = flip(x[...]).reshape(HEADS, HEAD_DIM, BLOCK)
        held[head] = out[head]

    def share_copy(i, out, held, ss, rs):
        to = lax.rem(head + i, HEADS)
        return copy(out.at[to], held.at[head], ss.at[i], rs.at[head], band=first + to)

    def share_arrival(i, out, held, ss, rs):
        src = lax.rem(head + HEADS - i, HEADS)
        return copy(out.at[0], held.at[src], ss.at[i], rs.at[src], band=first + src)

    k_args = (k_out, kt, k_ss, k_rs)
    v_args = (v_out, vt, v_ss, v_rs)
    q_args = (q_out, qt, q_ss, q_rs)
    g_args = (g_out, gt, g_ss, g_rs)

    spread(key, k_out, kt)
    pl.semaphore_wait(barrier, BANDS + 1)
    loop(1, BANDS, lambda d: spread_copy(d, *k_args).start())
    forward(band, kt, kf_ss, kf_rs).start()
    share(query, q_out, qt)
    loop(1, HEADS, lambda i: share_copy(i, *q_args).start())
    share(grad, g_out, gt)
    spread(value, v_out, vt)
    loop(1, BANDS, lambda d: relay(d, *k_args, kf_ss, kf_rs))
    loop(1, HEADS, lambda i: share_copy(i, *g_args).start())
    loop(1, BANDS, lambda d: spread_copy(d, *v_args).start())
    forward(band, vt, vf_ss, vf_rs).start()
    loop(1, HEADS, lambda i: share_arrival(i, *q_args).wait_recv())
    loop(0, BANDS, lambda src: forward(src, kt, kf_ss, kf_rs).wait_recv())

    def scores(t):
        q = flip(qt[t])
        state = [None]

        def step(j):
            x = dot(q, kt[ids[t, j]], 1, 0)
            s[:, COLS[j]] = x
            state[0] = join(state[0], fold(x, jnp.maximum), jnp.maximum)

        def finish():
            highest = jnp.max(state[0], axis=1, keepdims=True) * (SCALE * LOG2E)
            top[...] = jnp.broadcast_to(highest, (BLOCK, 128))

        return step, finish

    def exponentials(t):
        highest = top[:, :1]
        state = [None]

        def step(j):
            x = jnp.exp2(s[:, COLS[j]] * (SCALE * LOG2E) - highest)
            e[t, :, COLS[j]] = x.astype(bf16)
            state[0] = join(state[0], fold(x), jnp.add)

        def finish():
            inverse[t] = as_row(1.0 / jnp.sum(state[0], axis=1, keepdims=True))

        return step, finish

    def value_parts(t):
        gg = two_parts(gt[t].astype(f32) * inverse[t])

        def step(j):
            x = dot(gg, e[t, :, COLS[j]], 1, 0)
            parts[t, j] = x[:HEAD_DIM] + x[HEAD_DIM:]

        return step, lambda: None

    run_stages(scores(0))
    run_stages(exponentials(0), scores(1))
    loop(1, HEADS, lambda i: share_arrival(i, *g_args).wait_recv())

    def first_pass(p):
        loop(5 * p - 4, 5 * p + 1, lambda d: relay(d, *v_args, vf_ss, vf_rs))
        for t in (2 * p, 2 * p + 1):
            run_stages(exponentials(t - 1), scores(t), value_parts(t - 2))

    loop(1, TILES // 2, first_pass)
    run_stages(exponentials(TILES - 1), value_parts(TILES - 2))
    run_stages(value_parts(TILES - 1))

    def sum_blocks(b, n_out, n_in, ss, rs):
        sums = [None] * 4
        for t in range(TILES):
            x = parts[t, slots[t, b]]
            for c in range(4):
                sums[c] = join(sums[c], x * picks[t, 4 * b + c], jnp.add)
        for c in range(2):
            own[2 * b + c] = sums[c]
            n_out[2 * b + c] = sums[2 + c].astype(bf16)
        next_copy(b, n_out, n_in, ss, rs).start()

    def next_copy(b, n_out, n_in, ss, rs):
        return copy(
            n_out.at[pl.ds(2 * b, 2)], n_in.at[pl.ds(2 * b, 2)], ss.at[b], rs.at[b], cam=after
        )

    def return_copy(to, b_out, b_in, ss, rs):
        return copy(b_out.at[to], b_in.at[band], ss.at[to], rs.at[band], band=to)

    def return_arrival(d, b_out, b_in, ss, rs):
        src = behind(d)
        return copy(b_out.at[src], b_in.at[src], ss.at[src], rs.at[src], band=src)

    def total(b, n_args, b_out):
        next_copy(b, *n_args).wait_recv()
        n_in = n_args[1]
        b_out[b] = (own[pl.ds(2 * b, 2)] + n_in[pl.ds(2 * b, 2)].astype(f32)).astype(bf16)

    def give_back(d, n_args, b_args):
        to = ahead(d)
        total(to, n_args, b_args[0])
        return_copy(to, *b_args).start()

    def keep(n_args, b_out, b_in):
        total(band, n_args, b_out)
        b_in[band] = b_out[band]

    def assemble(b_in, out):
        for i in range(2):
            x = b_in[:HEADS, i].astype(f32) + b_in[HEADS:, i].astype(f32)
            x = x.reshape(HEADS * HEAD_DIM, BLOCK).T
            out[i * BLOCK : (i + 1) * BLOCK] = x.astype(bf16)

    vn_args = (n_out, vn_in, vn_ss, vn_rs)
    vb_args = (b_out, vb_in, vb_ss, vb_rs)
    kn_args = (n_out, kn_in, kn_ss, kn_rs)
    kb_args = (b_out, kb_in, kb_ss, kb_rs)

    loop(0, BANDS, lambda b: sum_blocks(b, *vn_args))
    loop(0, BANDS, lambda src: forward(src, vt, vf_ss, vf_rs).wait_recv())

    def dprobs(t):
        g = flip(gt[t])
        state = [None]

        def step(j):
            x = dot(g, vt[ids[t, j]], 1, 0)
            s[:, COLS[j]] = x
            state[0] = join(state[0], fold(e[t, :, COLS[j]].astype(f32) * x), jnp.add)

        def finish():
            scaled = jnp.broadcast_to(inverse[t], (128, BLOCK)).T
            delta[...] = jnp.sum(state[0], axis=1, keepdims=True) * scaled

        return step, finish

    def key_parts(t):
        qq = two_parts(qt[t].astype(f32) * inverse[t])
        shift = delta[:, :1]

        def step(j):
            ds = e[t, :, COLS[j]] * (s[:, COLS[j]] - shift).astype(bf16)
            x = dot(qq, ds, 1, 0)
            parts[t, j] = (x[:HEAD_DIM] + x[HEAD_DIM:]) * SCALE
            e[t, :, COLS[j]] = ds

        return step, lambda: None

    run_stages(dprobs(0))

    def second_pass(p):
        for t in (2 * p + 1, 2 * p + 2):
            run_stages(key_parts(t - 1), dprobs(t))
        loop(5 * p + 1, 5 * p + 6, lambda d: give_back(d, vn_args, vb_args))

    loop(0, TILES // 2 - 1, second_pass)
    keep(vn_args, b_out, vb_in)
    run_stages(key_parts(TILES - 2), dprobs(TILES - 1))
    run_stages(key_parts(TILES - 1))

    loop(0, BANDS, lambda b: next_copy(b, *vn_args).wait_send())
    loop(0, BANDS, lambda b: sum_blocks(b, *kn_args))

    def query_grad(i):
        t = lax.rem(head + i, HEADS)
        x = None
        for j in range(VIS):
            x = join(x, dot(e[t, :, COLS[j]], kt[ids[t, j]], 1, 1), jnp.add)
        dq_out[t] = (x.T * (inverse[t] * SCALE)).astype(bf16)

    def query_copy(i):
        t = lax.rem(head + i, HEADS)
        return copy(dq_out.at[t], dq_in.at[head], dq_ss.at[i], dq_rs.at[head], band=first + t)

    def query_arrival(i):
        src = lax.rem(head + HEADS - i, HEADS)
        return copy(dq_out.at[src], dq_in.at[src], dq_ss.at[i], dq_rs.at[src], band=first + src)

    def query_step(i):
        query_grad(i)
        query_copy(i).start()

    loop(1, 4, query_step)
    loop(1, BANDS, lambda d: return_copy(ahead(d), *vb_args).wait_send())
    loop(1, 6, lambda d: give_back(d, kn_args, kb_args))
    loop(4, 6, query_step)
    loop(6, 11, lambda d: give_back(d, kn_args, kb_args))
    loop(6, 8, query_step)
    loop(11, 16, lambda d: give_back(d, kn_args, kb_args))
    query_grad(0)
    dq_in[head] = dq_out[head]
    keep(kn_args, b_out, kb_in)

    loop(1, BANDS, lambda d: return_arrival(d, *vb_args).wait_recv())
    assemble(vb_in, d_value)
    loop(1, HEADS, lambda i: query_arrival(i).wait_recv())
    d_query[...] = dq_in[...].reshape(HEADS * HEAD_DIM, BLOCK).astype(f32).T.astype(bf16)
    loop(1, BANDS, lambda d: return_arrival(d, *kb_args).wait_recv())
    assemble(kb_in, d_key)

    def finish_band(d):
        spread_copy(d, *k_args).wait_send()
        spread_copy(d, *v_args).wait_send()
        return_copy(ahead(d), *kb_args).wait_send()

    def finish_cam(b):
        forward(b, kt, kf_ss, kf_rs).wait_send()
        forward(b, vt, vf_ss, vf_rs).wait_send()
        next_copy(b, *kn_args).wait_send()

    def finish_half(i):
        share_copy(i, *q_args).wait_send()
        share_copy(i, *g_args).wait_send()
        query_copy(i).wait_send()

    loop(1, BANDS, finish_band)
    loop(0, BANDS, finish_cam)
    loop(1, HEADS, finish_half)


def attention_grads(ids, slots, picks, query, key, value, grad):
    vmem = pl.BlockSpec(memory_space=pltpu.VMEM)
    smem = pl.BlockSpec(memory_space=pltpu.SMEM)

    def low(*shape):
        return pltpu.VMEM(shape, bf16)

    def full(*shape):
        return pltpu.VMEM(shape, f32)

    piece = (HEAD_DIM, BLOCK)
    dma = pltpu.SemaphoreType.DMA
    return pl.pallas_call(
        kernel,
        out_shape=[
            jax.ShapeDtypeStruct(query.shape, bf16),
            jax.ShapeDtypeStruct(key.shape, bf16),
            jax.ShapeDtypeStruct(value.shape, bf16),
        ],
        in_specs=[smem] * 3 + [vmem] * 4,
        out_specs=[vmem] * 3,
        scratch_shapes=[
            low(HEADS, 2, *piece), low(HEADS, 2, *piece), low(HEADS, *piece), low(HEADS, *piece),
            low(2 * BLOCKS, *piece), low(2 * BLOCKS, *piece), low(TILES, *piece), low(TILES, *piece),
            low(TILES, BLOCK, WIDE), full(BLOCK, WIDE), full(BLOCK, 128), full(BLOCK, 128),
            full(TILES, 1, BLOCK), full(TILES, VIS, *piece), full(BLOCKS, *piece),
        ]
        + [low(BLOCKS, *piece), low(BANDS, 2, *piece)]
        + [low(BLOCKS, *piece), low(BANDS, 2, *piece)] * 2
        + [low(TILES, *piece), low(TILES, *piece)]
        + [dma((BANDS,))] * 8
        + [dma((HEADS,))] * 4
        + [dma((BANDS,))] * 8
        + [dma((HEADS,))] * 2,
        compiler_params=pltpu.CompilerParams(
            collective_id=0, has_side_effects=True, vmem_limit_bytes=62 << 20
        ),
    )(ids, slots, picks, query, key, value, grad)


def local(query, key_img, value_img, d_out, visible):
    cam, band = lax.axis_index("cam"), lax.axis_index("band")
    start = cam * BANDS + band // TILES * TILES
    mine = lax.dynamic_slice_in_dim(visible, start, TILES, 0)
    offset = (mine // BLOCKS - cam) % CAMS
    ids = offset * BLOCKS + mine % BLOCKS
    hit = (mine % BLOCKS // 2)[:, None, :] == jnp.arange(BANDS)[None, :, None]
    slots = jnp.sum(jnp.where(hit, jnp.arange(VIS), 0), axis=2)
    choice = (offset * 2 + mine % 2)[:, None, None, :] == jnp.arange(4)[None, None, :, None]
    picks = jnp.sum((choice & hit[:, :, None]).astype(f32), axis=3).reshape(TILES, 4 * BANDS)
    d_query, d_key, d_value = attention_grads(
        ids, slots, picks, query, key_img[0], value_img[0], d_out
    )
    return d_query, d_key[None], d_value[None]


def solution(mesh):
    in_specs = (
        P(("cam", "band"), None),
        P("cam", "band", None),
        P("cam", "band", None),
        P(("cam", "band"), None),
        P(),
    )
    out_specs = (P(("cam", "band"), None), P("cam", "band", None), P("cam", "band", None))
    return jax.shard_map(local, mesh=mesh, in_specs=in_specs, out_specs=out_specs, check_vma=False)
```

time: 208 us -> 108 us (0.52)
  the two profiles are of different devices: /device:TPU:2 before, /device:TPU:1 now
where the time goes in v2:
time: 108 us; the launch traced here: 106 us
  Pallas kernels  98.4 us (91%)
  local copies, waits for them, and re-layouts  5.48 us (5%)
  other arithmetic  1.46 us (1%)
    pallas_call x1, Pallas kernels, attention_grads(): pl.pallas_call(kernel, out_shape=[jax.ShapeDtypeStruct(query.shape, bf16)...  98.4 us
    unnamed x10, local copies, waits for them, and re-layouts  4.5 us

profile of v2, /device:TPU:1, one launch (start us, length us, event | category | flops | bytes accessed | tf_op | source)
XLA Modules:
  0.0 106.1 jit_solution(8272412415663019644)
XLA Ops:
  0.6 0.0 copy-start
  0.7 0.7 copy-done
  1.3 0.1 constant_dynamic-slice_fusion
  1.4 0.1 copy.16
  1.5 0.6 fusion.3
  2.1 0.1 copy.13
  2.2 0.1 copy.12
  2.3 0.7 select_reduce_fusion.slots
  2.9 0.1 iota_compare_fusion
  3.0 0.1 convert_reduce_fusion
  3.1 0.1 copy.14
  3.2 0.7 copy.15.picks
  3.9 98.4 %shard_map.76 = (bf16[512,256]{1,0:T(8,128)(2,1)}, bf16[1024,256]{1,0:T(8,128)(2,1)}, bf16[1024,256]{1,0:T(8,128)(2,1)}) custom-call(s32[8,6]{1,0:T(8,128)} %get-tuple-element.10.ids, s32[8,16]{1,0:T(8,128)} %select_reduce_fusion.slots, f32[8,64]{1,0:T(8,128)} %copy.15.picks, bf16[512,256]{1,0:T(8,128)(2,1)} %query.1, bf16[1024,256]{1,0:T(8,128)(2,1)} %bitcast.5, ...), custom_call_target="tpu_custom_call" | custom-call | tf_op jit(solution)/shard_map/pallas_call | solution.py:382
  102.3 0.0 copy-start.2
  102.3 1.7 %copy.20 = bf16[512,256]{1,0:T(8,128)(2,1)} copy(bf16[512,256]{1,0:T(8,128)(2,1)} %get-tuple-element.15) | data formatting | bytes 524288
  104.1 0.0 copy-done.2
  104.1 0.0 copy-start.1
  104.1 0.8 copy.21
  104.9 0.4 copy-done.1
  105.3 0.8 copy.22
  (1 shorter events, 0.0 us)
Async XLA Ops:
  0.6 0.7 copy-start
  102.3 1.7 %copy-start.2 = (bf16[1024,256]{1,0:T(8,128)(2,1)S(1)}, bf16[1024,256]{1,0:T(8,128)(2,1)}, u32[]{:S(2)}) copy-start(bf16[1024,256]{1,0:T(8,128)(2,1)} %get-tuple-element.7) | copy-start | bytes 1572868
  104.1 1.2 %copy-start.1 = (bf16[1024,256]{1,0:T(8,128)(2,1)S(1)}, bf16[1024,256]{1,0:T(8,128)(2,1)}, u32[]{:S(2)}) copy-start(bf16[1024,256]{1,0:T(8,128)(2,1)} %get-tuple-element.8) | copy-start | bytes 1572868

commit v3 on v2

--- a/solution.py
+++ b/solution.py
@@ -13,6 +13,7 @@
 HEAD_DIM = 32
 TILES = 8
 BANDS = 16
+SIDE = 4
 CAMS = 8
 BLOCKS = 2 * BANDS
 WIDE = VIS * BLOCK
@@ -67,11 +68,11 @@
 
 
 def kernel(
-    ids, slots, picks, query, key, value, grad,
+    visible, query, key, value, grad,
     d_query, d_key, d_value,
     k_out, v_out, q_out, g_out,
     kt, vt, qt, gt,
-    e, s, top, delta, inverse, parts, own,
+    ids, slots, picks, e, s, top, delta, inverse, parts, own,
     n_out, b_out, vn_in, vb_in, kn_in, kb_in,
     dq_out, dq_in,
     k_ss, k_rs, kf_ss, kf_rs, v_ss, v_rs, vf_ss, vf_rs,
@@ -90,11 +91,18 @@
             device_id=where, device_id_type=pl.DeviceIdType.MESH,
         )
 
+    def reach(d, sign):
+        z, y = lax.div(d, SIDE), lax.rem(d, SIDE)
+        z, y = (r + lax.div(r, 2) * (5 - 2 * r) for r in (z, y))
+        z = lax.rem(lax.div(band, SIDE) + sign * z + SIDE, SIDE)
+        y = lax.rem(lax.rem(band, SIDE) + sign * y + SIDE, SIDE)
+        return z * SIDE + y
+
     def ahead(d):
-        return lax.rem(band + d, BANDS)
+        return reach(jnp.int32(d), 1)
 
     def behind(d):
-        return lax.rem(band + BANDS - d, BANDS)
+        return reach(jnp.int32(d), -1)
 
     barrier = pltpu.get_barrier_semaphore()
 
@@ -145,6 +153,28 @@
     def share_arrival(i, out, held, ss, rs):
         src = lax.rem(head + HEADS - i, HEADS)
         return copy(out.at[0], held.at[src], ss.at[i], rs.at[src], band=first + src)
+
+    def make_tables():
+        def one_tile(t):
+            band_of, choice = [], []
+            for j in range(VIS):
+                block = visible[cam * BANDS + first + t, j]
+                place = lax.rem(block, BLOCKS)
+                offset = (lax.div(block, BLOCKS) != cam).astype(jnp.int32)
+                ids[t, j] = offset * BLOCKS + place
+                band_of.append(lax.div(place, 2))
+                choice.append(2 * offset + lax.rem(place, 2))
+
+            def one_band(b):
+                hit = [(x == b).astype(jnp.int32) for x in band_of]
+                slots[t, b] = functools.reduce(jnp.maximum, [j * hit[j] for j in range(1, VIS)])
+                for c in range(4):
+                    match = sum(h * (x == c).astype(jnp.int32) for h, x in zip(hit, choice))
+                    picks[t, 4 * b + c] = match.astype(f32)
+
+            loop(0, BANDS, one_band)
+
+        loop(0, TILES, one_tile)
 
     k_args = (k_out, kt, k_ss, k_rs)
     v_args = (v_out, vt, v_ss, v_rs)
@@ -159,10 +189,11 @@
     loop(1, HEADS, lambda i: share_copy(i, *q_args).start())
     share(grad, g_out, gt)
     spread(value, v_out, vt)
-    loop(1, BANDS, lambda d: relay(d, *k_args, kf_ss, kf_rs))
     loop(1, HEADS, lambda i: share_copy(i, *g_args).start())
     loop(1, BANDS, lambda d: spread_copy(d, *v_args).start())
     forward(band, vt, vf_ss, vf_rs).start()
+    make_tables()
+    loop(1, BANDS, lambda d: relay(d, *k_args, kf_ss, kf_rs))
     loop(1, HEADS, lambda i: share_arrival(i, *q_args).wait_recv())
     loop(0, BANDS, lambda src: forward(src, kt, kf_ss, kf_rs).wait_recv())
 
@@ -209,8 +240,13 @@
     loop(1, HEADS, lambda i: share_arrival(i, *g_args).wait_recv())
 
     def first_pass(p):
-        loop(5 * p - 4, 5 * p + 1, lambda d: relay(d, *v_args, vf_ss, vf_rs))
-        for t in (2 * p, 2 * p + 1):
+        for half in range(2):
+            t = 2 * p + half
+            low = 8 * (p - 1) + 4 * half + 1
+            loop(
+                jnp.minimum(low, BANDS), jnp.minimum(low + 4, BANDS),
+                lambda d: relay(d, *v_args, vf_ss, vf_rs),
+            )
             run_stages(exponentials(t - 1), scores(t), value_parts(t - 2))
 
     loop(1, TILES // 2, first_pass)
@@ -245,8 +281,8 @@
         n_in = n_args[1]
         b_out[b] = (own[pl.ds(2 * b, 2)] + n_in[pl.ds(2 * b, 2)].astype(f32)).astype(bf16)
 
-    def give_back(d, n_args, b_args):
-        to = ahead(d)
+    def give_back(i, n_args, b_args):
+        to = ahead(BANDS - i)
         total(to, n_args, b_args[0])
         return_copy(to, *b_args).start()
 
@@ -265,7 +301,7 @@
     kn_args = (n_out, kn_in, kn_ss, kn_rs)
     kb_args = (b_out, kb_in, kb_ss, kb_rs)
 
-    loop(0, BANDS, lambda b: sum_blocks(b, *vn_args))
+    loop(0, BANDS, lambda i: sum_blocks(ahead(BANDS - 1 - i), *vn_args))
     loop(0, BANDS, lambda src: forward(src, vt, vf_ss, vf_rs).wait_recv())
 
     def dprobs(t):
@@ -308,7 +344,7 @@
     run_stages(key_parts(TILES - 1))
 
     loop(0, BANDS, lambda b: next_copy(b, *vn_args).wait_send())
-    loop(0, BANDS, lambda b: sum_blocks(b, *kn_args))
+    loop(0, BANDS, lambda i: sum_blocks(ahead(BANDS - 1 - i), *kn_args))
 
     def query_grad(i):
         t = lax.rem(head + i, HEADS)
@@ -329,15 +365,17 @@
         query_grad(i)
         query_copy(i).start()
 
+    loop(1, BANDS, lambda d: return_copy(ahead(d), *vb_args).wait_send())
     loop(1, 4, query_step)
-    loop(1, BANDS, lambda d: return_copy(ahead(d), *vb_args).wait_send())
-    loop(1, 6, lambda d: give_back(d, kn_args, kb_args))
-    loop(4, 6, query_step)
-    loop(6, 11, lambda d: give_back(d, kn_args, kb_args))
-    loop(6, 8, query_step)
-    loop(11, 16, lambda d: give_back(d, kn_args, kb_args))
+
+    def query_steps(i):
+        query_step(i)
+        loop(2 * i - 7, 2 * i - 5, lambda d: give_back(d, kn_args, kb_args))
+
+    loop(4, HEADS, query_steps)
     query_grad(0)
     dq_in[head] = dq_out[head]
+    loop(9, BANDS, lambda d: give_back(d, kn_args, kb_args))
     keep(kn_args, b_out, kb_in)
 
     loop(1, BANDS, lambda d: return_arrival(d, *vb_args).wait_recv())
@@ -367,7 +405,7 @@
     loop(1, HEADS, finish_half)
 
 
-def attention_grads(ids, slots, picks, query, key, value, grad):
+def attention_grads(visible, query, key, value, grad):
     vmem = pl.BlockSpec(memory_space=pltpu.VMEM)
     smem = pl.BlockSpec(memory_space=pltpu.SMEM)
 
@@ -386,11 +424,13 @@
             jax.ShapeDtypeStruct(key.shape, bf16),
             jax.ShapeDtypeStruct(value.shape, bf16),
         ],
-        in_specs=[smem] * 3 + [vmem] * 4,
+        in_specs=[smem] + [vmem] * 4,
         out_specs=[vmem] * 3,
         scratch_shapes=[
             low(HEADS, 2, *piece), low(HEADS, 2, *piece), low(HEADS, *piece), low(HEADS, *piece),
             low(2 * BLOCKS, *piece), low(2 * BLOCKS, *piece), low(TILES, *piece), low(TILES, *piece),
+            pltpu.SMEM((TILES, VIS), jnp.int32), pltpu.SMEM((TILES, BANDS), jnp.int32),
+            pltpu.SMEM((TILES, 4 * BANDS), f32),
             low(TILES, BLOCK, WIDE), full(BLOCK, WIDE), full(BLOCK, 128), full(BLOCK, 128),
             full(TILES, 1, BLOCK), full(TILES, VIS, *piece), full(BLOCKS, *piece),
         ]
@@ -404,21 +444,12 @@
         compiler_params=pltpu.CompilerParams(
             collective_id=0, has_side_effects=True, vmem_limit_bytes=62 << 20
         ),
-    )(ids, slots, picks, query, key, value, grad)
+    )(visible, query, key, value, grad)
 
 
 def local(query, key_img, value_img, d_out, visible):
-    cam, band = lax.axis_index("cam"), lax.axis_index("band")
-    start = cam * BANDS + band // TILES * TILES
-    mine = lax.dynamic_slice_in_dim(visible, start, TILES, 0)
-    offset = (mine // BLOCKS - cam) % CAMS
-    ids = offset * BLOCKS + mine % BLOCKS
-    hit = (mine % BLOCKS // 2)[:, None, :] == jnp.arange(BANDS)[None, :, None]
-    slots = jnp.sum(jnp.where(hit, jnp.arange(VIS), 0), axis=2)
-    choice = (offset * 2 + mine % 2)[:, None, None, :] == jnp.arange(4)[None, None, :, None]
-    picks = jnp.sum((choice & hit[:, :, None]).astype(f32), axis=3).reshape(TILES, 4 * BANDS)
     d_query, d_key, d_value = attention_grads(
-        ids, slots, picks, query, key_img[0], value_img[0], d_out
+        visible, query, key_img[0], value_img[0], d_out
     )
     return d_query, d_key[None], d_value[None]
 

time: 108 us -> 103 us (0.954); the launches traced: 106 us -> 103 us
  Pallas kernels: 98.4 us -> 96.8 us
  other arithmetic: 1.46 us -> 0 us
    pallas_call x1, Pallas kernels: 98.4 us -> 96.8 us  [attention_grads(): pl.pallas_call(kernel, out_shape=[jax.ShapeDtypeStruct(query.shape, bf16)...]
    unnamed x10 -> x8, local copies, waits for them, and re-layouts: 4.5 us -> 5.18 us
where the time goes in v3:
time: 103 us
  Pallas kernels  96.8 us (94%)
  local copies, waits for them, and re-layouts  5.18 us (5%)
    pallas_call x1, Pallas kernels, attention_grads(): pl.pallas_call(kernel, out_shape=[jax.ShapeDtypeStruct(query.shape, bf16)...  96.8 us
    unnamed x8, local copies, waits for them, and re-layouts  5.18 us

profile of v3, /device:TPU:1, one launch (start us, length us, event | category | flops | bytes accessed | tf_op | source)
XLA Modules:
  0.0 102.7 jit_solution(6403469662504123292)
XLA Ops:
  0.6 1.4 %copy.8.visible = s32[128,6]{1,0:T(8,128)} copy(s32[128,6]{0,1:T(8,128)} %param.9) | data formatting | bytes 6144 | tf_op args[4]
  2.1 96.8 %shard_map.76 = (bf16[512,256]{1,0:T(8,128)(2,1)}, bf16[1024,256]{1,0:T(8,128)(2,1)}, bf16[1024,256]{1,0:T(8,128)(2,1)}) custom-call(s32[128,6]{1,0:T(8,128)} %copy.8.visible, bf16[512,256]{1,0:T(8,128)(2,1)} %query.1, bf16[1024,256]{1,0:T(8,128)(2,1)} %bitcast.4, bf16[1024,256]{1,0:T(8,128)(2,1)} %bitcast.5, bf16[512,256]{1,0:T(8,128)(2,1)} %grad.1), custom_call_target="tpu_custom_call" | custom-call | tf_op jit(solution)/shard_map/pallas_call | solution.py:420
  98.9 0.0 copy-start.1
  98.9 1.7 %copy.12 = bf16[512,256]{1,0:T(8,128)(2,1)} copy(bf16[512,256]{1,0:T(8,128)(2,1)} %get-tuple-element.12) | data formatting | bytes 524288
  100.6 0.0 copy-done.1
  100.6 0.0 copy-start
  100.6 0.8 copy.13
  101.4 0.4 copy-done
  101.9 0.8 copy.14
Async XLA Ops:
  98.9 1.7 %copy-start.1 = (bf16[1024,256]{1,0:T(8,128)(2,1)S(1)}, bf16[1024,256]{1,0:T(8,128)(2,1)}, u32[]{:S(2)}) copy-start(bf16[1024,256]{1,0:T(8,128)(2,1)} %get-tuple-element.7) | copy-start | bytes 1572868
  100.6 1.2 %copy-start = (bf16[1024,256]{1,0:T(8,128)(2,1)S(1)}, bf16[1024,256]{1,0:T(8,128)(2,1)}, u32[]{:S(2)}) copy-start(bf16[1024,256]{1,0:T(8,128)(2,1)} %get-tuple-element.8) | copy-start | bytes 1572868

commit v4 on v3

--- a/solution.py
+++ b/solution.py
@@ -68,9 +68,10 @@
 
 
 def kernel(
-    visible, query, key, value, grad,
-    d_query, d_key, d_value,
-    k_out, v_out, q_out, g_out,
+    visible, query_hbm, key_hbm, value_hbm, grad_hbm,
+    d_query_hbm, d_key_hbm, d_value_hbm,
+    query, key, value, grad, d_query, d_key, d_value, load_sem, store_sem,
+    kv_out, q_out, g_out,
     kt, vt, qt, gt,
     ids, slots, picks, e, s, top, delta, inverse, parts, own,
     n_out, b_out, vn_in, vb_in, kn_in, kb_in,
@@ -104,6 +105,19 @@
     def behind(d):
         return reach(jnp.int32(d), -1)
 
+    def load(i):
+        src, dst = ((key_hbm, key), (query_hbm, query), (grad_hbm, grad), (value_hbm, value))[i]
+        return pltpu.make_async_copy(src, dst, load_sem.at[i])
+
+    def store(i):
+        src, dst = ((d_value, d_value_hbm), (d_query, d_query_hbm), (d_key, d_key_hbm))[i]
+        return pltpu.make_async_copy(src, dst, store_sem.at[i])
+
+    def all_done(ref, sem):
+        pltpu.make_async_copy(ref, ref, sem.at[0]).wait()
+
+    for i in range(4):
+        load(i).start()
     barrier = pltpu.get_barrier_semaphore()
 
     def greet(d):
@@ -125,17 +139,17 @@
     def spread_copy(d, out, held, ss, rs):
         to = ahead(d)
         return copy(
-            out.at[lax.rem(to, HEADS)], held.at[pl.ds(2 * band, 2)], ss.at[d], rs.at[band], band=to
+            out.at[lax.rem(to, HEADS)], held.at[pl.ds(2 * band, 2)], ss.at[0], rs.at[band], band=to
         )
 
     def arrival(d, out, held, ss, rs):
         src = behind(d)
-        return copy(out.at[0], held.at[pl.ds(2 * src, 2)], ss.at[d], rs.at[src], band=ahead(d))
+        return copy(out.at[0], held.at[pl.ds(2 * src, 2)], ss.at[0], rs.at[src], band=ahead(d))
 
     def forward(src, held, ss, rs):
         return copy(
             held.at[pl.ds(2 * src, 2)], held.at[pl.ds(BLOCKS + 2 * src, 2)],
-            ss.at[src], rs.at[src], cam=before,
+            ss.at[0], rs.at[0], cam=before,
         )
 
     def relay(d, out, held, ss, rs, fss, frs):
@@ -148,17 +162,13 @@
 
     def share_copy(i, out, held, ss, rs):
         to = lax.rem(head + i, HEADS)
-        return copy(out.at[to], held.at[head], ss.at[i], rs.at[head], band=first + to)
-
-    def share_arrival(i, out, held, ss, rs):
-        src = lax.rem(head + HEADS - i, HEADS)
-        return copy(out.at[0], held.at[src], ss.at[i], rs.at[src], band=first + src)
+        return copy(out.at[to], held.at[head], ss.at[0], rs.at[0], band=first + to)
 
     def make_tables():
         def one_tile(t):
             band_of, choice = [], []
             for j in range(VIS):
-                block = visible[cam * BANDS + first + t, j]
+                block = visible[j, cam * BANDS + first + t]
                 place = lax.rem(block, BLOCKS)
                 offset = (lax.div(block, BLOCKS) != cam).astype(jnp.int32)
                 ids[t, j] = offset * BLOCKS + place
@@ -176,26 +186,32 @@
 
         loop(0, TILES, one_tile)
 
+    k_out, v_out = kv_out.at[pl.ds(0, HEADS)], kv_out.at[pl.ds(HEADS, HEADS)]
     k_args = (k_out, kt, k_ss, k_rs)
     v_args = (v_out, vt, v_ss, v_rs)
     q_args = (q_out, qt, q_ss, q_rs)
     g_args = (g_out, gt, g_ss, g_rs)
 
+    load(0).wait()
     spread(key, k_out, kt)
     pl.semaphore_wait(barrier, BANDS + 1)
     loop(1, BANDS, lambda d: spread_copy(d, *k_args).start())
     forward(band, kt, kf_ss, kf_rs).start()
+    load(1).wait()
     share(query, q_out, qt)
+    load(2).wait()
+    share(grad, g_out, gt)
+    load(3).wait()
+    spread(value, v_out, vt)
+    make_tables()
+    loop(1, 9, lambda d: relay(d, *k_args, kf_ss, kf_rs))
     loop(1, HEADS, lambda i: share_copy(i, *q_args).start())
-    share(grad, g_out, gt)
-    spread(value, v_out, vt)
     loop(1, HEADS, lambda i: share_copy(i, *g_args).start())
     loop(1, BANDS, lambda d: spread_copy(d, *v_args).start())
     forward(band, vt, vf_ss, vf_rs).start()
-    make_tables()
-    loop(1, BANDS, lambda d: relay(d, *k_args, kf_ss, kf_rs))
-    loop(1, HEADS, lambda i: share_arrival(i, *q_args).wait_recv())
-    loop(0, BANDS, lambda src: forward(src, kt, kf_ss, kf_rs).wait_recv())
+    loop(9, BANDS, lambda d: relay(d, *k_args, kf_ss, kf_rs))
+    all_done(qt.at[pl.ds(0, HEADS - 1)], q_rs)
+    all_done(kt.at[pl.ds(0, BLOCKS)], kf_rs)
 
     def scores(t):
         q = flip(qt[t])
@@ -237,7 +253,7 @@
 
     run_stages(scores(0))
     run_stages(exponentials(0), scores(1))
-    loop(1, HEADS, lambda i: share_arrival(i, *g_args).wait_recv())
+    all_done(gt.at[pl.ds(0, HEADS - 1)], g_rs)
 
     def first_pass(p):
         for half in range(2):
@@ -266,15 +282,11 @@
 
     def next_copy(b, n_out, n_in, ss, rs):
         return copy(
-            n_out.at[pl.ds(2 * b, 2)], n_in.at[pl.ds(2 * b, 2)], ss.at[b], rs.at[b], cam=after
+            n_out.at[pl.ds(2 * b, 2)], n_in.at[pl.ds(2 * b, 2)], ss.at[0], rs.at[b], cam=after
         )
 
     def return_copy(to, b_out, b_in, ss, rs):
-        return copy(b_out.at[to], b_in.at[band], ss.at[to], rs.at[band], band=to)
-
-    def return_arrival(d, b_out, b_in, ss, rs):
-        src = behind(d)
-        return copy(b_out.at[src], b_in.at[src], ss.at[src], rs.at[src], band=src)
+        return copy(b_out.at[to], b_in.at[band], ss.at[0], rs.at[0], band=to)
 
     def total(b, n_args, b_out):
         next_copy(b, *n_args).wait_recv()
@@ -299,10 +311,12 @@
     vn_args = (n_out, vn_in, vn_ss, vn_rs)
     vb_args = (b_out, vb_in, vb_ss, vb_rs)
     kn_args = (n_out, kn_in, kn_ss, kn_rs)
-    kb_args = (b_out, kb_in, kb_ss, kb_rs)
+    kb_args = (kv_out, kb_in, kb_ss, kb_rs)
 
     loop(0, BANDS, lambda i: sum_blocks(ahead(BANDS - 1 - i), *vn_args))
-    loop(0, BANDS, lambda src: forward(src, vt, vf_ss, vf_rs).wait_recv())
+    all_done(vt.at[pl.ds(0, BLOCKS)], vf_rs)
+    for sem in (k_ss, v_ss):
+        all_done(kt.at[pl.ds(0, BLOCKS - 2)], sem)
 
     def dprobs(t):
         g = flip(gt[t])
@@ -336,14 +350,16 @@
     def second_pass(p):
         for t in (2 * p + 1, 2 * p + 2):
             run_stages(key_parts(t - 1), dprobs(t))
-        loop(5 * p + 1, 5 * p + 6, lambda d: give_back(d, vn_args, vb_args))
+        loop(
+            jnp.maximum(8 * p - 7, 1), jnp.minimum(8 * p + 1, BANDS),
+            lambda d: give_back(d, vn_args, vb_args),
+        )
 
     loop(0, TILES // 2 - 1, second_pass)
-    keep(vn_args, b_out, vb_in)
     run_stages(key_parts(TILES - 2), dprobs(TILES - 1))
     run_stages(key_parts(TILES - 1))
-
-    loop(0, BANDS, lambda b: next_copy(b, *vn_args).wait_send())
+    keep(vn_args, b_out, vb_in)
+    all_done(n_out, vn_ss)
     loop(0, BANDS, lambda i: sum_blocks(ahead(BANDS - 1 - i), *kn_args))
 
     def query_grad(i):
@@ -355,17 +371,12 @@
 
     def query_copy(i):
         t = lax.rem(head + i, HEADS)
-        return copy(dq_out.at[t], dq_in.at[head], dq_ss.at[i], dq_rs.at[head], band=first + t)
-
-    def query_arrival(i):
-        src = lax.rem(head + HEADS - i, HEADS)
-        return copy(dq_out.at[src], dq_in.at[src], dq_ss.at[i], dq_rs.at[src], band=first + src)
+        return copy(dq_out.at[t], dq_in.at[head], dq_ss.at[0], dq_rs.at[0], band=first + t)
 
     def query_step(i):
         query_grad(i)
         query_copy(i).start()
 
-    loop(1, BANDS, lambda d: return_copy(ahead(d), *vb_args).wait_send())
     loop(1, 4, query_step)
 
     def query_steps(i):
@@ -376,37 +387,29 @@
     query_grad(0)
     dq_in[head] = dq_out[head]
     loop(9, BANDS, lambda d: give_back(d, kn_args, kb_args))
-    keep(kn_args, b_out, kb_in)
-
-    loop(1, BANDS, lambda d: return_arrival(d, *vb_args).wait_recv())
+    keep(kn_args, kv_out, kb_in)
+
+    all_done(vb_in.at[pl.ds(0, BANDS - 1)], vb_rs)
     assemble(vb_in, d_value)
-    loop(1, HEADS, lambda i: query_arrival(i).wait_recv())
+    store(0).start()
+    all_done(dq_in.at[pl.ds(0, HEADS - 1)], dq_rs)
     d_query[...] = dq_in[...].reshape(HEADS * HEAD_DIM, BLOCK).astype(f32).T.astype(bf16)
-    loop(1, BANDS, lambda d: return_arrival(d, *kb_args).wait_recv())
+    store(1).start()
+    for sem in (kf_ss, vf_ss, kn_ss):
+        all_done(kt.at[pl.ds(0, BLOCKS)], sem)
+    for sem in (q_ss, g_ss, dq_ss):
+        all_done(qt.at[pl.ds(0, HEADS - 1)], sem)
+    all_done(kb_in.at[pl.ds(0, BANDS - 1)], kb_rs)
     assemble(kb_in, d_key)
-
-    def finish_band(d):
-        spread_copy(d, *k_args).wait_send()
-        spread_copy(d, *v_args).wait_send()
-        return_copy(ahead(d), *kb_args).wait_send()
-
-    def finish_cam(b):
-        forward(b, kt, kf_ss, kf_rs).wait_send()
-        forward(b, vt, vf_ss, vf_rs).wait_send()
-        next_copy(b, *kn_args).wait_send()
-
-    def finish_half(i):
-        share_copy(i, *q_args).wait_send()
-        share_copy(i, *g_args).wait_send()
-        query_copy(i).wait_send()
-
-    loop(1, BANDS, finish_band)
-    loop(0, BANDS, finish_cam)
-    loop(1, HEADS, finish_half)
+    store(2).start()
+    for sem in (vb_ss, kb_ss):
+        all_done(b_out.at[pl.ds(0, BANDS - 1)], sem)
+    for i in range(3):
+        store(i).wait()
 
 
 def attention_grads(visible, query, key, value, grad):
-    vmem = pl.BlockSpec(memory_space=pltpu.VMEM)
+    hbm = pl.BlockSpec(memory_space=pl.ANY)
     smem = pl.BlockSpec(memory_space=pltpu.SMEM)
 
     def low(*shape):
@@ -424,10 +427,12 @@
             jax.ShapeDtypeStruct(key.shape, bf16),
             jax.ShapeDtypeStruct(value.shape, bf16),
         ],
-        in_specs=[smem] + [vmem] * 4,
-        out_specs=[vmem] * 3,
-        scratch_shapes=[
-            low(HEADS, 2, *piece), low(HEADS, 2, *piece), low(HEADS, *piece), low(HEADS, *piece),
+        in_specs=[smem] + [hbm] * 4,
+        out_specs=[hbm] * 3,
+        scratch_shapes=[low(*x.shape) for x in (query, key, value, grad, query, key, value)]
+        + [dma((4,)), dma((3,))]
+        + [
+            low(BANDS, 2, *piece), low(HEADS, *piece), low(HEADS, *piece),
             low(2 * BLOCKS, *piece), low(2 * BLOCKS, *piece), low(TILES, *piece), low(TILES, *piece),
             pltpu.SMEM((TILES, VIS), jnp.int32), pltpu.SMEM((TILES, BANDS), jnp.int32),
             pltpu.SMEM((TILES, 4 * BANDS), f32),
@@ -437,10 +442,7 @@
         + [low(BLOCKS, *piece), low(BANDS, 2, *piece)]
         + [low(BLOCKS, *piece), low(BANDS, 2, *piece)] * 2
         + [low(TILES, *piece), low(TILES, *piece)]
-        + [dma((BANDS,))] * 8
-        + [dma((HEADS,))] * 4
-        + [dma((BANDS,))] * 8
-        + [dma((HEADS,))] * 2,
+        + [dma((n,)) for n in (1, BANDS, 1, 1) * 2 + (1,) * 4 + (1, BANDS, 1, 1) * 2 + (1, 1)],
         compiler_params=pltpu.CompilerParams(
             collective_id=0, has_side_effects=True, vmem_limit_bytes=62 << 20
         ),
@@ -449,7 +451,7 @@
 
 def local(query, key_img, value_img, d_out, visible):
     d_query, d_key, d_value = attention_grads(
-        visible, query, key_img[0], value_img[0], d_out
+        visible.T, query, key_img[0], value_img[0], d_out
     )
     return d_query, d_key[None], d_value[None]
 

time: 103 us -> 99.9 us (0.970); the launches traced: 103 us -> 98.5 us
  Pallas kernels: 96.8 us -> 94.1 us
  local copies, waits for them, and re-layouts: 5.18 us -> 3.75 us
    pallas_call x1, Pallas kernels: 96.8 us -> 94.1 us  [attention_grads(): pl.pallas_call(kernel, out_shape=[jax.ShapeDtypeStruct(query.shape, bf16)...]
    unnamed x8 -> x7, local copies, waits for them, and re-layouts: 5.18 us -> 3.75 us
where the time goes in v4:
time: 99.9 us; the launch traced here: 98.5 us
  Pallas kernels  94.1 us (94%)
  local copies, waits for them, and re-layouts  3.75 us (4%)
    pallas_call x1, Pallas kernels, attention_grads(): pl.pallas_call(kernel, out_shape=[jax.ShapeDtypeStruct(query.shape, bf16)...  94.1 us
    unnamed x7, local copies, waits for them, and re-layouts  3.75 us

profile of v4, /device:TPU:1, one launch (start us, length us, event | category | flops | bytes accessed | tf_op | source)
XLA Modules:
  0.0 98.5 jit_solution(2777631015687456062)
XLA Ops:
  0.6 94.1 %shard_map.76 = (bf16[512,256]{1,0:T(8,128)(2,1)}, bf16[1024,256]{1,0:T(8,128)(2,1)}, bf16[1024,256]{1,0:T(8,128)(2,1)}) custom-call(s32[6,128]{1,0:T(8,128)} %bitcast.9, bf16[512,256]{1,0:T(8,128)(2,1)} %query_hbm.1, bf16[1024,256]{1,0:T(8,128)(2,1)} %bitcast.5, bf16[1024,256]{1,0:T(8,128)(2,1)} %bitcast.6, bf16[512,256]{1,0:T(8,128)(2,1)} %grad_hbm.1), custom_call_target="tpu_custom_call" | custom-call | tf_op jit(solution)/shard_map/pallas_call | solution.py:423
  94.7 0.0 copy-start.1
  94.7 1.7 %copy.11 = bf16[512,256]{1,0:T(8,128)(2,1)} copy(bf16[512,256]{1,0:T(8,128)(2,1)} %get-tuple-element.12) | data formatting | bytes 524288
  96.5 0.0 copy-done.1
  96.5 0.0 copy-start
  96.5 0.8 copy.12
  97.3 0.4 copy-done
  97.7 0.8 copy.13
Async XLA Ops:
  94.7 1.7 %copy-start.1 = (bf16[1024,256]{1,0:T(8,128)(2,1)S(1)}, bf16[1024,256]{1,0:T(8,128)(2,1)}, u32[]{:S(2)}) copy-start(bf16[1024,256]{1,0:T(8,128)(2,1)} %get-tuple-element.7) | copy-start | bytes 1572868
  96.5 1.2 %copy-start = (bf16[1024,256]{1,0:T(8,128)(2,1)S(1)}, bf16[1024,256]{1,0:T(8,128)(2,1)}, u32[]{:S(2)}) copy-start(bf16[1024,256]{1,0:T(8,128)(2,1)} %get-tuple-element.8) | copy-start | bytes 1572868

commit v5 on v4

--- a/solution.py
+++ b/solution.py
@@ -51,6 +51,11 @@
     return new if old is None else op(old, new)
 
 
+def join_heads(x):
+    x = x[:HEADS].astype(f32) + x[HEADS:].astype(f32)
+    return x.reshape(HEADS * HEAD_DIM, BLOCK).T.astype(bf16)
+
+
 def run_stages(*stages):
     for j in range(VIS):
         for step, _ in stages:
@@ -69,12 +74,12 @@
 
 def kernel(
     visible, query_hbm, key_hbm, value_hbm, grad_hbm,
-    d_query_hbm, d_key_hbm, d_value_hbm,
-    query, key, value, grad, d_query, d_key, d_value, load_sem, store_sem,
+    d_query_hbm, kb_in, d_value_hbm,
+    query, key, value, grad, d_query, d_value, load_sem, store_sem,
     kv_out, q_out, g_out,
     kt, vt, qt, gt,
     ids, slots, picks, e, s, top, delta, inverse, parts, own,
-    n_out, b_out, vn_in, vb_in, kn_in, kb_in,
+    n_out, b_out, vn_in, vb_in, kn_in,
     dq_out, dq_in,
     k_ss, k_rs, kf_ss, kf_rs, v_ss, v_rs, vf_ss, vf_rs,
     q_ss, q_rs, g_ss, g_rs,
@@ -110,7 +115,7 @@
         return pltpu.make_async_copy(src, dst, load_sem.at[i])
 
     def store(i):
-        src, dst = ((d_value, d_value_hbm), (d_query, d_query_hbm), (d_key, d_key_hbm))[i]
+        src, dst = ((d_value, d_value_hbm), (d_query, d_query_hbm), (kv_out.at[band], kb_in.at[band]))[i]
         return pltpu.make_async_copy(src, dst, store_sem.at[i])
 
     def all_done(ref, sem):
@@ -258,9 +263,9 @@
     def first_pass(p):
         for half in range(2):
             t = 2 * p + half
-            low = 8 * (p - 1) + 4 * half + 1
+            low = 6 * (p - 1) + 3 * half + 1
             loop(
-                jnp.minimum(low, BANDS), jnp.minimum(low + 4, BANDS),
+                jnp.minimum(low, BANDS), jnp.minimum(low + 3, BANDS),
                 lambda d: relay(d, *v_args, vf_ss, vf_rs),
             )
             run_stages(exponentials(t - 1), scores(t), value_parts(t - 2))
@@ -298,16 +303,6 @@
         total(to, n_args, b_args[0])
         return_copy(to, *b_args).start()
 
-    def keep(n_args, b_out, b_in):
-        total(band, n_args, b_out)
-        b_in[band] = b_out[band]
-
-    def assemble(b_in, out):
-        for i in range(2):
-            x = b_in[:HEADS, i].astype(f32) + b_in[HEADS:, i].astype(f32)
-            x = x.reshape(HEADS * HEAD_DIM, BLOCK).T
-            out[i * BLOCK : (i + 1) * BLOCK] = x.astype(bf16)
-
     vn_args = (n_out, vn_in, vn_ss, vn_rs)
     vb_args = (b_out, vb_in, vb_ss, vb_rs)
     kn_args = (n_out, kn_in, kn_ss, kn_rs)
@@ -348,17 +343,20 @@
     run_stages(dprobs(0))
 
     def second_pass(p):
-        for t in (2 * p + 1, 2 * p + 2):
+        for half in range(2):
+            t = 2 * p + half + 1
             run_stages(key_parts(t - 1), dprobs(t))
-        loop(
-            jnp.maximum(8 * p - 7, 1), jnp.minimum(8 * p + 1, BANDS),
-            lambda d: give_back(d, vn_args, vb_args),
-        )
+            low = 3 * t - 2
+            loop(
+                jnp.minimum(low, BANDS), jnp.minimum(low + 3, BANDS),
+                lambda i: give_back(i, vn_args, vb_args),
+            )
 
     loop(0, TILES // 2 - 1, second_pass)
     run_stages(key_parts(TILES - 2), dprobs(TILES - 1))
     run_stages(key_parts(TILES - 1))
-    keep(vn_args, b_out, vb_in)
+    total(band, vn_args, b_out)
+    vb_in[band] = b_out[band]
     all_done(n_out, vn_ss)
     loop(0, BANDS, lambda i: sum_blocks(ahead(BANDS - 1 - i), *kn_args))
 
@@ -387,10 +385,12 @@
     query_grad(0)
     dq_in[head] = dq_out[head]
     loop(9, BANDS, lambda d: give_back(d, kn_args, kb_args))
-    keep(kn_args, kv_out, kb_in)
+    total(band, kn_args, kv_out)
+    store(2).start()
 
     all_done(vb_in.at[pl.ds(0, BANDS - 1)], vb_rs)
-    assemble(vb_in, d_value)
+    for i in range(2):
+        d_value[i * BLOCK : (i + 1) * BLOCK] = join_heads(vb_in[:, i])
     store(0).start()
     all_done(dq_in.at[pl.ds(0, HEADS - 1)], dq_rs)
     d_query[...] = dq_in[...].reshape(HEADS * HEAD_DIM, BLOCK).astype(f32).T.astype(bf16)
@@ -399,13 +399,27 @@
         all_done(kt.at[pl.ds(0, BLOCKS)], sem)
     for sem in (q_ss, g_ss, dq_ss):
         all_done(qt.at[pl.ds(0, HEADS - 1)], sem)
-    all_done(kb_in.at[pl.ds(0, BANDS - 1)], kb_rs)
-    assemble(kb_in, d_key)
-    store(2).start()
-    for sem in (vb_ss, kb_ss):
+    for sem in (vb_ss, kb_ss, kb_rs):
         all_done(b_out.at[pl.ds(0, BANDS - 1)], sem)
     for i in range(3):
         store(i).wait()
+
+
+def last_kernel(query_in, sums, value_in, d_query, d_key, d_value):
+    for i in range(2):
+        d_key[i * BLOCK : (i + 1) * BLOCK] = join_heads(sums[:, i])
+    d_query[...] = query_in[...]
+    d_value[...] = value_in[...]
+
+
+def last_step(d_query, sums, d_value):
+    vmem = pl.BlockSpec(memory_space=pltpu.VMEM)
+    return pl.pallas_call(
+        last_kernel,
+        out_shape=[jax.ShapeDtypeStruct(x.shape, bf16) for x in (d_query, d_value, d_value)],
+        in_specs=[vmem] * 3,
+        out_specs=[vmem] * 3,
+    )(d_query, sums, d_value)
 
 
 def attention_grads(visible, query, key, value, grad):
@@ -424,12 +438,12 @@
         kernel,
         out_shape=[
             jax.ShapeDtypeStruct(query.shape, bf16),
-            jax.ShapeDtypeStruct(key.shape, bf16),
+            jax.ShapeDtypeStruct((BANDS, 2, *piece), bf16),
             jax.ShapeDtypeStruct(value.shape, bf16),
         ],
         in_specs=[smem] + [hbm] * 4,
         out_specs=[hbm] * 3,
-        scratch_shapes=[low(*x.shape) for x in (query, key, value, grad, query, key, value)]
+        scratch_shapes=[low(*x.shape) for x in (query, key, value, grad, query, value)]
         + [dma((4,)), dma((3,))]
         + [
             low(BANDS, 2, *piece), low(HEADS, *piece), low(HEADS, *piece),
@@ -440,7 +454,7 @@
             full(TILES, 1, BLOCK), full(TILES, VIS, *piece), full(BLOCKS, *piece),
         ]
         + [low(BLOCKS, *piece), low(BANDS, 2, *piece)]
-        + [low(BLOCKS, *piece), low(BANDS, 2, *piece)] * 2
+        + [low(BLOCKS, *piece), low(BANDS, 2, *piece), low(BLOCKS, *piece)]
         + [low(TILES, *piece), low(TILES, *piece)]
         + [dma((n,)) for n in (1, BANDS, 1, 1) * 2 + (1,) * 4 + (1, BANDS, 1, 1) * 2 + (1, 1)],
         compiler_params=pltpu.CompilerParams(
@@ -450,9 +464,8 @@
 
 
 def local(query, key_img, value_img, d_out, visible):
-    d_query, d_key, d_value = attention_grads(
-        visible.T, query, key_img[0], value_img[0], d_out
-    )
+    d_query, sums, d_value = attention_grads(visible.T, query, key_img[0], value_img[0], d_out)
+    d_query, d_key, d_value = last_step(d_query, sums, d_value)
     return d_query, d_key[None], d_value[None]
 
 

time: 99.9 us -> 95.1 us (0.952)
  local copies, waits for them, and re-layouts: 3.75 us -> 0 us
  Pallas kernels: 94.1 us -> 92.6 us
    pallas_call x1, Pallas kernels: 94.1 us -> 90 us  [attention_grads(): pl.pallas_call(kernel, out_shape=[jax.ShapeDtypeStruct(query.shape, bf16)...]
    unnamed x7 -> x0, local copies, waits for them, and re-layouts: 3.75 us -> none
    pallas_call x0 -> x1, Pallas kernels: none -> 2.66 us  [last_step(): pl.pallas_call(last_kernel, out_shape=[jax.ShapeDtypeStruct(x.shape, bf16...]
where the time goes in v5:
time: 95.1 us; the launch traced here: 93.3 us
  Pallas kernels  92.6 us (97%)
    pallas_call x1, Pallas kernels, attention_grads(): pl.pallas_call(kernel, out_shape=[jax.ShapeDtypeStruct(query.shape, bf16)...  90 us
    pallas_call x1, Pallas kernels, last_step(): pl.pallas_call(last_kernel, out_shape=[jax.ShapeDtypeStruct(x.shape, bf16...  2.66 us

profile of v5, /device:TPU:1, one launch (start us, length us, event | category | flops | bytes accessed | tf_op | source)
XLA Modules:
  0.0 93.3 jit_solution(3700226350778194419)
XLA Ops:
  0.6 90.0 %shard_map.76 = (bf16[512,256]{1,0:T(8,128)(2,1)}, bf16[16,2,32,512]{3,2,1,0:T(8,128)(2,1)}, bf16[1024,256]{1,0:T(8,128)(2,1)}) custom-call(s32[6,128]{1,0:T(8,128)} %bitcast.7, bf16[512,256]{1,0:T(8,128)(2,1)} %query_hbm.1, bf16[1024,256]{1,0:T(8,128)(2,1)} %bitcast.5, bf16[1024,256]{1,0:T(8,128)(2,1)} %bitcast.6, bf16[512,256]{1,0:T(8,128)(2,1)} %grad_hbm.1), custom_call_target="tpu_custom_call" | custom-call | tf_op jit(solution)/shard_map/pallas_call | solution.py:437
  90.6 2.7 %shard_map.77 = (bf16[512,256]{1,0:T(8,128)(2,1)}, bf16[1024,256]{1,0:T(8,128)(2,1)}, bf16[1024,256]{1,0:T(8,128)(2,1)}) custom-call(bf16[512,256]{1,0:T(8,128)(2,1)} %get-tuple-element.9.query_in, bf16[16,2,32,512]{3,2,1,0:T(8,128)(2,1)} %get-tuple-element.10.sums, bf16[1024,256]{1,0:T(8,128)(2,1)} %get-tuple-element.11.value_in), custom_call_target="tpu_custom_call" | custom-call | tf_op jit(solution)/shard_map/pallas_call | solution.py:417

commit v6 on v5

--- a/solution.py
+++ b/solution.py
@@ -263,9 +263,9 @@
     def first_pass(p):
         for half in range(2):
             t = 2 * p + half
-            low = 6 * (p - 1) + 3 * half + 1
+            low = 8 * (p - 1) + 4 * half - 3
             loop(
-                jnp.minimum(low, BANDS), jnp.minimum(low + 3, BANDS),
+                jnp.clip(low, 1, BANDS), jnp.clip(low + 4, 1, BANDS),
                 lambda d: relay(d, *v_args, vf_ss, vf_rs),
             )
             run_stages(exponentials(t - 1), scores(t), value_parts(t - 2))
@@ -340,17 +340,20 @@
 
         return step, lambda: None
 
+    late = 1 + (BANDS - 1) * lax.rem(cam, 2)
+
+    def give_range(low, high, n_args, b_args):
+        low, high = (jnp.minimum(jnp.maximum(x, late), BANDS) for x in (low, high))
+        loop(low, high, lambda i: give_back(i, n_args, b_args))
+
+    loop(1, late, lambda i: give_back(i, vn_args, vb_args))
     run_stages(dprobs(0))
 
     def second_pass(p):
         for half in range(2):
             t = 2 * p + half + 1
             run_stages(key_parts(t - 1), dprobs(t))
-            low = 3 * t - 2
-            loop(
-                jnp.minimum(low, BANDS), jnp.minimum(low + 3, BANDS),
-                lambda i: give_back(i, vn_args, vb_args),
-            )
+            give_range(3 * t - 2, 3 * t + 1, vn_args, vb_args)
 
     loop(0, TILES // 2 - 1, second_pass)
     run_stages(key_parts(TILES - 2), dprobs(TILES - 1))
@@ -375,16 +378,17 @@
         query_grad(i)
         query_copy(i).start()
 
+    loop(1, late, lambda i: give_back(i, kn_args, kb_args))
     loop(1, 4, query_step)
 
     def query_steps(i):
         query_step(i)
-        loop(2 * i - 7, 2 * i - 5, lambda d: give_back(d, kn_args, kb_args))
+        give_range(2 * i - 7, 2 * i - 5, kn_args, kb_args)
 
     loop(4, HEADS, query_steps)
     query_grad(0)
     dq_in[head] = dq_out[head]
-    loop(9, BANDS, lambda d: give_back(d, kn_args, kb_args))
+    give_range(9, BANDS, kn_args, kb_args)
     total(band, kn_args, kv_out)
     store(2).start()
 

time: 95.1 us -> 91.8 us (0.965); the launches traced: 93.3 us -> 91.6 us
  Pallas kernels: 92.6 us -> 91 us
    pallas_call x1, Pallas kernels: 90 us -> 88.3 us  [attention_grads(): pl.pallas_call(kernel, out_shape=[jax.ShapeDtypeStruct(query.shape, bf16)...]
where the time goes in v6:
time: 91.8 us; the launch traced here: 91.6 us
  Pallas kernels  91 us (99%)
    pallas_call x1, Pallas kernels, attention_grads(): pl.pallas_call(kernel, out_shape=[jax.ShapeDtypeStruct(query.shape, bf16)...  88.3 us
    pallas_call x1, Pallas kernels, last_step(): pl.pallas_call(last_kernel, out_shape=[jax.ShapeDtypeStruct(x.shape, bf16...  2.66 us

profile of v6, /device:TPU:1, one launch (start us, length us, event | category | flops | bytes accessed | tf_op | source)
XLA Modules:
  0.0 91.6 jit_solution(3296719343833393531)
XLA Ops:
  0.6 88.3 %shard_map.76 = (bf16[512,256]{1,0:T(8,128)(2,1)}, bf16[16,2,32,512]{3,2,1,0:T(8,128)(2,1)}, bf16[1024,256]{1,0:T(8,128)(2,1)}) custom-call(s32[6,128]{1,0:T(8,128)} %bitcast.7, bf16[512,256]{1,0:T(8,128)(2,1)} %query_hbm.1, bf16[1024,256]{1,0:T(8,128)(2,1)} %bitcast.5, bf16[1024,256]{1,0:T(8,128)(2,1)} %bitcast.6, bf16[512,256]{1,0:T(8,128)(2,1)} %grad_hbm.1), custom_call_target="tpu_custom_call" | custom-call | tf_op jit(solution)/shard_map/pallas_call | solution.py:441
  89.0 2.7 %shard_map.77 = (bf16[512,256]{1,0:T(8,128)(2,1)}, bf16[1024,256]{1,0:T(8,128)(2,1)}, bf16[1024,256]{1,0:T(8,128)(2,1)}) custom-call(bf16[512,256]{1,0:T(8,128)(2,1)} %get-tuple-element.9.query_in, bf16[16,2,32,512]{3,2,1,0:T(8,128)(2,1)} %get-tuple-element.10.sums, bf16[1024,256]{1,0:T(8,128)(2,1)} %get-tuple-element.11.value_in), custom_call_target="tpu_custom_call" | custom-call | tf_op jit(solution)/shard_map/pallas_call | solution.py:421

commit v7 on v6

--- a/solution.py
+++ b/solution.py
@@ -64,12 +64,12 @@
         finish()
 
 
-def loop(low, high, body):
+def loop(low, high, body, unroll=1):
     def step(i, _):
         body(i)
         return None
 
-    lax.fori_loop(low, high, step, None)
+    lax.fori_loop(low, high, step, None, unroll=unroll) if unroll > 1 else lax.fori_loop(low, high, step, None)
 
 
 def kernel(
@@ -308,7 +308,7 @@
     kn_args = (n_out, kn_in, kn_ss, kn_rs)
     kb_args = (kv_out, kb_in, kb_ss, kb_rs)
 
-    loop(0, BANDS, lambda i: sum_blocks(ahead(BANDS - 1 - i), *vn_args))
+    loop(0, BANDS, lambda i: sum_blocks(ahead(BANDS - 1 - i), *vn_args), 4)
     all_done(vt.at[pl.ds(0, BLOCKS)], vf_rs)
     for sem in (k_ss, v_ss):
         all_done(kt.at[pl.ds(0, BLOCKS - 2)], sem)
@@ -361,7 +361,7 @@
     total(band, vn_args, b_out)
     vb_in[band] = b_out[band]
     all_done(n_out, vn_ss)
-    loop(0, BANDS, lambda i: sum_blocks(ahead(BANDS - 1 - i), *kn_args))
+    loop(0, BANDS, lambda i: sum_blocks(ahead(BANDS - 1 - i), *kn_args), 4)
 
     def query_grad(i):
         t = lax.rem(head + i, HEADS)

time: 91.8 us -> 91.6 us (level)
  no operation moved by 1% of the time
where the time goes in v7:
time: 91.6 us; the launch traced here: 91.4 us
  Pallas kernels  90.7 us (99%)
    pallas_call x1, Pallas kernels, attention_grads(): pl.pallas_call(kernel, out_shape=[jax.ShapeDtypeStruct(query.shape, bf16)...  88.1 us
    pallas_call x1, Pallas kernels, last_step(): pl.pallas_call(last_kernel, out_shape=[jax.ShapeDtypeStruct(x.shape, bf16...  2.66 us

profile of v7, /device:TPU:1, one launch (start us, length us, event | category | flops | bytes accessed | tf_op | source)
XLA Modules:
  0.0 91.4 jit_solution(2934392082627515693)
XLA Ops:
  0.6 88.1 %shard_map.76 = (bf16[512,256]{1,0:T(8,128)(2,1)}, bf16[16,2,32,512]{3,2,1,0:T(8,128)(2,1)}, bf16[1024,256]{1,0:T(8,128)(2,1)}) custom-call(s32[6,128]{1,0:T(8,128)} %bitcast.7, bf16[512,256]{1,0:T(8,128)(2,1)} %query_hbm.1, bf16[1024,256]{1,0:T(8,128)(2,1)} %bitcast.5, bf16[1024,256]{1,0:T(8,128)(2,1)} %bitcast.6, bf16[512,256]{1,0:T(8,128)(2,1)} %grad_hbm.1), custom_call_target="tpu_custom_call" | custom-call | tf_op jit(solution)/shard_map/pallas_call | solution.py:441
  88.7 2.7 %shard_map.77 = (bf16[512,256]{1,0:T(8,128)(2,1)}, bf16[1024,256]{1,0:T(8,128)(2,1)}, bf16[1024,256]{1,0:T(8,128)(2,1)}) custom-call(bf16[512,256]{1,0:T(8,128)(2,1)} %get-tuple-element.9.query_in, bf16[16,2,32,512]{3,2,1,0:T(8,128)(2,1)} %get-tuple-element.10.sums, bf16[1024,256]{1,0:T(8,128)(2,1)} %get-tuple-element.11.value_in), custom_call_target="tpu_custom_call" | custom-call | tf_op jit(solution)/shard_map/pallas_call | solution.py:421
